TPU v7x, 512 devices: a whole 4x4x16 slice. The times are simulated.
512 devices in a mesh: grp: 16 (over z), dev: 32 (over y, x, core).
Axes of the slice: x: 4, y: 4, z: 16, core: 2. Of those that a mesh axis runs over, the one named last changes fastest.
Arguments:
- records: bfloat16 [2048, 2, 2048], P(('grp', 'dev')), may hold values from -40 to 40
- partners: int32 [2048, 16], P(('grp', 'dev')), may hold values from 0 to 2047, as said below
- routes: int32 [2048, 2], P(('grp', 'dev')), may hold values from 0 to 15, all different within a row; in each aligned block of 4 rows (0 to 3, 4 to 7, ...) at most 2 rows name the same one
Outputs:
- near_corr: bfloat16 [2048, 16, 2048], P(('grp', 'dev'))
- far_corr: bfloat16 [16, 32, 32, 4, 2048], P('grp', 'dev')
Inputs may be any that keep to these rules, and one draw needn't show every extreme that they name: partners[c, q] lies in the same segment of 128 channels as c, differs from c, and at most 16 channels away; every channel has partners exactly 16 below or above it. `routes`: each channel names 2 different groups; of the 4 channels of one device at most 2 name the same group, and some device reaches 2.
All inputs are finite; a program needn't handle non-finite values.
Results may differ from a plain program's by a relative error of at most 0.0081.
Values may be sent and summed in bfloat16 or wider, within the bound.
No kernel may reach another device: no remote copies, remote signals or barrier semaphores. Data moves between devices by JAX's collectives and lax.ppermute only.
A program may use at most 64 MiB of HBM per device.

v0:
```python
import math

import jax
import jax.numpy as jnp
import numpy as np
from jax import lax
from jax.experimental import pallas as pl
from jax.experimental.pallas import tpu as pltpu
from jax.sharding import PartitionSpec as P

NT = 2048
BINS = 1024
LANES = 128
ROWS = 32
C = math.sqrt(0.5)
COLS = ((0, 128), (256, 384), (512, 768), (640, 896), (1024, 1280), (1152, 1408), (1536, 1792), (1664, 1920))
F32, BF16 = jnp.float32, jnp.bfloat16


def make_tables():
    b = np.arange(256)
    k = np.arange(128)

    def trig(bins):
        angle = (b[:, None] * bins[None, :]) % NT * (2.0 * np.pi / NT)
        return np.cos(angle), np.sin(angle)

    tiles = [np.concatenate([cos, -sin], axis=1) for cos, sin in (trig(8 * k), trig(8 * k + 4))]
    for r in (2, 1, 3):
        tiles += trig(np.concatenate([8 * k + r, -(8 * k + 8 - r)]))

    def stacked(tiles):
        cut = [tile[:, lo : lo + LANES] for tile in tiles for lo in (0, LANES)]
        return np.concatenate(cut, axis=0).astype(np.float32).astype(jnp.bfloat16)

    return stacked(tiles + [tile.T for tile in tiles])


TILES = 8
VMEM_LIMIT = 60 * 1024 * 1024


def dot(a, b):
    return jnp.dot(a, b, preferred_element_type=F32)


def fetch(pairs, sems):
    moves = [pltpu.make_async_copy(src, dst, sems.at[m]) for m, (src, dst) in enumerate(pairs)]
    for move in moves:
        move.start()
    return moves


def tile(table_ref, m):
    return jnp.concatenate([table_ref[pl.ds(512 * m, 256), :], table_ref[pl.ds(512 * m + 256, 256), :]], axis=1)


def products(one_ref, two_ref, y_ref, n, table_ref, first, sign):
    for m in range(2):
        y_ref[0:n, 256 * m : 256 * (m + 1)] = dot(one_ref[m], tile(table_ref, first + m))
    for m in range(3):
        c = dot(two_ref[m], tile(table_ref, first + 2 + 2 * m))
        s = dot(two_ref[m], tile(table_ref, first + 3 + 2 * m))
        col = 512 * (m + 1)
        re, im = (c[:n] + s[n:], c[n:] - s[:n]) if sign == 1 else (c[:n] - s[n:], c[n:] + s[:n])
        y_ref[0:n, col : col + 256] = re
        y_ref[0:n, col + 256 : col + 512] = im


def select_kernel(routes_hbm, own_hbm, out_ref, routes_ref, own_ref, sems):
    for move in fetch([(routes_hbm, routes_ref), (own_hbm, own_ref)], sems):
        move.wait()
    for h in range(16):
        hit = [(routes_ref[0, i] == h) | (routes_ref[1, i] == h) for i in range(4)]
        count = sum(x.astype(jnp.int32) for x in hit)
        first = jnp.where(hit[0], 0, jnp.where(hit[1], 1, jnp.where(hit[2], 2, 3)))
        last = jnp.where(hit[3], 3, jnp.where(hit[2], 2, jnp.where(hit[1], 1, 0)))
        for k, pick in ((0, first), (1, last)):
            rows = own_ref[pl.ds(pl.multiple_of(pick * ROWS, ROWS), ROWS), :]
            out_ref[pl.ds((2 * h + k) * ROWS, ROWS), :] = jnp.where(count > k, rows, jnp.zeros_like(rows))


def spread(x_ref, stride, start, blk_ref, count):
    for c in range(count):
        x_ref[pl.ds((start + c) * stride, ROWS), :] = blk_ref[pl.ds(c * ROWS, ROWS), :].astype(F32)


def forward(x_ref, stride, n, one_ref, two_ref, z_ref, table_ref, move):
    for w in range(2):
        for half in range(2):
            x = [x_ref[pl.ds(2 * (2 * a + half) + w, n, stride=stride), :] for a in range(8)]
            s = [x[a] + x[a + 4] for a in range(4)]
            d = [x[a] - x[a + 4] for a in range(4)]
            even, odd = s[0] + s[2], s[1] + s[3]
            diff, summ = C * (d[1] - d[3]), C * (d[1] + d[3])
            lanes = pl.ds(half * LANES, LANES)
            for m, part in enumerate((even + odd, even - odd)):
                one_ref[m, pl.ds(w * n, n), lanes] = part.astype(BF16)
            for m, parts in enumerate(
                ((s[0] - s[2], s[3] - s[1]), (d[0] + diff, -d[2] - summ), (d[0] - diff, d[2] - summ))
            ):
                for k, part in enumerate(parts):
                    two_ref[m, pl.ds((2 * k + w) * n, n), lanes] = part.astype(BF16)
    move.wait()
    products(one_ref, two_ref, z_ref, 2 * n, table_ref, 0, 1)
    total = None
    for re, im in COLS:
        zr, zi = z_ref[0 : 2 * n, re : re + LANES], z_ref[0 : 2 * n, im : im + LANES]
        energy = zr * zr + zi * zi
        total = energy if total is None else total + energy
    return jnp.sum(total, axis=1, keepdims=True) * (1.0 / BINS)


def whitened(z_ref, level, re, im):
    n = level.shape[0]
    zr, zi = z_ref[0:n, re : re + LANES], z_ref[0:n, im : im + LANES]
    scale = lax.rsqrt(zr * zr + zi * zi + level)
    return zr * scale, zi * scale


def put(one_ref, two_ref, chunk, lo, sr, si):
    n = sr.shape[0]
    sr, si = (sr * (1.0 / 64)).astype(BF16), (si * (1.0 / 64)).astype(BF16)
    if chunk < 2:
        one_ref[chunk, pl.ds(lo, n), 0:LANES] = sr
        one_ref[chunk, pl.ds(lo, n), LANES : 2 * LANES] = si
    else:
        rows = two_ref.shape[1] // 2
        m, lanes = (chunk - 2) // 2, pl.ds(chunk % 2 * LANES, LANES)
        two_ref[m, pl.ds(lo, n), lanes] = sr
        two_ref[m, pl.ds(rows + lo, n), lanes] = si


def lags(h_ref, lo, n, half):
    p0, p4, a2, b2, a1, b1, a3, b3 = (
        h_ref[lo : lo + n, 256 * m + half * LANES : 256 * m + (half + 1) * LANES] for m in range(8)
    )
    even, odd = p0 + p4, p0 - p4
    plus, minus = even + a2, even - a2
    a13, b31 = a1 + a3, b3 - b1
    low, high = odd - b2, odd + b2
    t1, t3 = C * (a1 - b1 - a3 - b3), C * (a3 - b3 - a1 - b1)
    return (plus + a13, low + t1, minus + b31, high + t3, plus - a13, low - t1, minus - b31, high - t3)


NEAR, FAR, N = 48, 32, 80
STRIDE = 40
PAIRS, SLOT = 64 + 4 * FAR, 72
GROUP = 8


def picked(dev, partners_ref):
    core = dev % 2
    col = lax.broadcasted_iota(jnp.int32, (64, NEAR), 1)
    row = lax.broadcasted_iota(jnp.int32, (64, NEAR), 0)
    wanted = jnp.zeros((64, NEAR), jnp.int32)
    for c in range(4):
        for q in range(16):
            wanted = jnp.where(row == c * 16 + q, partners_ref[c, q] & 127, wanted)
    block = col // 8
    step = jnp.where(block == 1, -1, jnp.where(block == 2, -2, jnp.where(block == 3, 1, jnp.where(block == 4, 2, 0))))
    flip = jnp.where(block >= 3, 1, 0)
    in_core = (core + flip + (col // 4) % 2) % 2
    ids = 8 * (dev // 2 + (1 - 2 * core) * step) + in_core * 4 + col % 4
    ids = jnp.where(block < 5, ids, -1)
    return jnp.where(wanted == ids, 1.0, 0.0).astype(BF16)


def correlate_kernel(dev_ref, partners_hbm, *refs):
    near_hbm, (recv_hbm, table_hbm, near_out, far_out), refs = refs[:5], refs[5:9], refs[9:]
    near_refs, (recv_ref, table_ref, partners_ref), refs = refs[:5], refs[5:8], refs[8:]
    x_ref, u1_ref, u2_ref, z_ref, w_ref, p_ref, s1_ref, s2_ref, h_ref, o_ref, near_ref, far_ref, sems, out_sems = refs
    half = 512 * TILES
    moves = fetch(
        [
            (table_hbm.at[pl.ds(0, half), :], table_ref.at[pl.ds(0, half), :]),
            *zip(near_hbm, near_refs),
            (recv_hbm, recv_ref),
            (partners_hbm, partners_ref),
            (table_hbm.at[pl.ds(half, half), :], table_ref.at[pl.ds(half, half), :]),
        ],
        sems,
    )
    x_ref[pl.ds(40 * STRIDE, 8 * STRIDE), :] = jnp.zeros((8 * STRIDE, LANES), F32)
    for move in moves[1:8]:
        move.wait()
    for m, ref in enumerate(near_refs):
        spread(x_ref, STRIDE, 8 * m, ref, 8)
    spread(x_ref, STRIDE, NEAR, recv_ref, FAR)
    level = 0.1 * forward(x_ref, STRIDE, N, u1_ref, u2_ref, z_ref, table_ref, moves[0]) + 1e-6
    for chunk, (re, im) in enumerate(COLS):
        wr, wi = whitened(z_ref, level, re, im)
        for w in range(2):
            w_ref[w, :, re : re + LANES] = wr[w * N : w * N + NEAR].astype(BF16)
            w_ref[w, :, im : im + LANES] = wi[w * N : w * N + NEAR].astype(BF16)
        for i in range(4):
            sr = si = 0.0
            for w in range(2):
                at = w * N + NEAR
                fr, fi = wr[at : at + FAR], wi[at : at + FAR]
                br, bi = wr[w * N + i : w * N + i + 1], wi[w * N + i : w * N + i + 1]
                sr = sr + (fr * br + fi * bi)
                si = si + (fi * br - fr * bi)
            put(s1_ref, s2_ref, chunk, 64 + i * FAR, sr, si)
    picker = picked(dev_ref[0], partners_ref)
    for w in range(2):
        p_ref[w] = dot(picker, w_ref[w])
    for chunk, (re, im) in enumerate(COLS):
        own = [[w_ref[w, 0:16, k : k + LANES].astype(F32) for k in (re, im)] for w in range(2)]
        for c in range(4):
            sr = si = 0.0
            for w in range(2):
                pr, pi = (p_ref[w, c * 16 : (c + 1) * 16, k : k + LANES] for k in (re, im))
                ar, ai = own[w][0][c : c + 1], own[w][1][c : c + 1]
                sr = sr + (ar * pr + ai * pi)
                si = si + (ai * pr - ar * pi)
            put(s1_ref, s2_ref, chunk, c * 16, sr, si)
    moves[8].wait()
    products(s1_ref, s2_ref, h_ref, PAIRS, table_ref, TILES, -1)
    for lo in range(0, 64, 16):
        for part in range(2):
            for a, lag in enumerate(lags(h_ref, lo, 16, part)):
                at = 256 * a + LANES * part
                near_ref[lo : lo + 16, at : at + LANES] = lag.astype(BF16)
    outs = [pltpu.make_async_copy(near_ref, near_out, out_sems.at[0])]
    outs[0].start()
    for g in range(FAR // GROUP):
        for i in range(4):
            for part in range(2):
                for a, lag in enumerate(lags(h_ref, 64 + i * FAR + g * GROUP, GROUP, part)):
                    o_ref[pl.ds(g * GROUP * SLOT + (2 * a + part) * 4 + i, GROUP, stride=SLOT), :] = lag
        for s in range(g * GROUP, (g + 1) * GROUP):
            far_ref[pl.ds(s * 64, 64), :] = o_ref[pl.ds(s * SLOT, 64), :].astype(BF16)
        rows = pl.ds(g * GROUP * 64, GROUP * 64)
        outs.append(pltpu.make_async_copy(far_ref.at[rows, :], far_out.at[rows, :], out_sems.at[1 + g]))
        outs[-1].start()
    for out in outs:
        out.wait()


def vmem():
    return pl.BlockSpec(memory_space=pltpu.VMEM)


def smem():
    return pl.BlockSpec(memory_space=pltpu.SMEM)


def hbm():
    return pl.BlockSpec(memory_space=pltpu.HBM)


def like(*shape):
    return jax.ShapeDtypeStruct(shape, BF16)


def shards(records, partners, routes):
    table = jnp.asarray(make_tables())
    members = lax.axis_size("dev")
    swap = [(d, d ^ 1) for d in range(members)]

    def toward(chips):
        pairs = [(d, d + (2 * chips if d % 2 == 0 else -2 * chips)) for d in range(members)]
        return [(s, t) for s, t in pairs if 0 <= t < members]

    raw = records.reshape(4, 2, 16, LANES).transpose(0, 2, 1, 3).reshape(4 * ROWS, LANES)
    outgoing = pl.pallas_call(
        select_kernel,
        out_shape=like(32 * ROWS, LANES),
        in_specs=[hbm(), hbm()],
        out_specs=vmem(),
        scratch_shapes=[
            pltpu.SMEM((2, 4), jnp.int32),
            pltpu.VMEM((4 * ROWS, LANES), BF16),
            pltpu.SemaphoreType.DMA((2,)),
        ],
        name="select",
    )(routes.T, raw)
    other = lax.ppermute(raw, "dev", swap)
    outgoing, other = lax.optimization_barrier((outgoing, other))
    arrived = lax.all_to_all(outgoing.reshape(16, 2 * ROWS, LANES), "grp", 0, 0, tiled=True).reshape(32 * ROWS, LANES)

    chip = jnp.concatenate([raw, other], axis=0)
    one_side = lax.ppermute(chip, "dev", toward(1))
    two_side = lax.ppermute(chip, "dev", toward(2))
    one_far = lax.ppermute(one_side, "dev", swap)
    two_far = lax.ppermute(two_side, "dev", swap)
    dev = lax.axis_index("dev").astype(jnp.int32).reshape(1)
    blocks = (chip, one_side, two_side, one_far, two_far)
    near, far = pl.pallas_call(
        correlate_kernel,
        out_shape=(like(64, NT), like(64 * FAR, LANES)),
        in_specs=[smem()] + [hbm()] * 8,
        out_specs=(hbm(), hbm()),
        scratch_shapes=[pltpu.VMEM(x.shape, BF16) for x in (*blocks, arrived, table)]
        + [
            pltpu.SMEM((4, 16), jnp.int32),
            pltpu.VMEM((N * STRIDE, LANES), F32),
            pltpu.VMEM((2, 2 * N, 256), BF16),
            pltpu.VMEM((3, 4 * N, 256), BF16),
            pltpu.VMEM((2 * N, NT), F32),
            pltpu.VMEM((2, NEAR, NT), BF16),
            pltpu.VMEM((2, 64, NT), F32),
            pltpu.VMEM((2, PAIRS, 256), BF16),
            pltpu.VMEM((3, 2 * PAIRS, 256), BF16),
            pltpu.VMEM((PAIRS, NT), F32),
            pltpu.VMEM((FAR * SLOT, LANES), F32),
            pltpu.VMEM((64, NT), BF16),
            pltpu.VMEM((64 * FAR, LANES), BF16),
            pltpu.SemaphoreType.DMA((9,)),
            pltpu.SemaphoreType.DMA((1 + FAR // GROUP,)),
        ],
        compiler_params=pltpu.CompilerParams(vmem_limit_bytes=VMEM_LIMIT),
        name="correlate",
    )(dev, partners, *blocks, arrived, table)
    far = far.reshape(32, 16, 4, LANES).transpose(0, 2, 1, 3).reshape(1, 1, 32, 4, NT)
    return (near.reshape(4, 16, NT), far)


def solution(mesh):
    placed = (P(("grp", "dev"), None, None), P(("grp", "dev"), None), P(("grp", "dev"), None))
    return jax.shard_map(
        shards,
        mesh=mesh,
        in_specs=placed,
        out_specs=(P(("grp", "dev"), None, None), P("grp", "dev", None, None, None)),
        check_vma=False,
    )
```

profile of v0, /device:TPU:26, one launch (start us, length us, event | category | flops | bytes accessed | tf_op | source)
XLA Modules:
  0.0 44.0 jit_solution(11796741293089735751)
XLA Ops:
  0.6 1.9 %collective-permute-start = (bf16[128,128]{1,0:T(8,128)(2,1)}, bf16[128,128]{1,0:T(8,128)(2,1)S(1)}, u32[]{:S(2)}, u32[]{:S(2)}) collective-permute-start(bf16[128,128]{1,0:T(8,128)(2,1)} %bitcast.17), channel_id=1, source_target_pairs={{0,1},{1,0},{2,3},{3,2},{4,5},{5,4},{6,7},{7,6},{8,9},{9,8},{10,11... | collective-permute-start | bytes 98312 | tf_op jit(solution)/shard_map/ppermute | solution.py:279
  2.6 1.7 %select.1 = bf16[1024,128]{1,0:T(8,128)(2,1)} custom-call(s32[2,4]{1,0:T(2,128)} %bitcast.20, bf16[128,128]{1,0:T(8,128)(2,1)} %bitcast.18), custom_call_target="tpu_custom_call" | custom-call | tf_op jit(solution)/shard_map/select/pallas_call | solution.py:267
  4.2 0.0 collective-permute-done
  4.3 15.2 %all-to-all-start = ((bf16[16,64,128]{2,1,0:T(8,128)(2,1)}), bf16[16,64,128]{2,1,0:T(8,128)(2,1)S(1)}, u32[]{:S(2)}, u32[]{:S(2)}) async-start(bf16[16,64,128]{2,1,0:T(8,128)(2,1)} %bitcast.16), calls=%async_computation | async-start | bytes 524288 | tf_op jit(solution)/shard_map/all_to_all | solution.py:281
  19.5 0.8 %pad_maximum_fusion.refs_0_ = bf16[256,128]{1,0:T(8,128)(2,1)S(1)} fusion(bf16[128,128]{1,0:T(8,128)(2,1)S(1)} %collective-permute-done, bf16[128,128]{1,0:T(8,128)(2,1)} %bitcast.19), kind=kLoop, calls=%fused_computation | loop fusion | flops 131072 | bytes 131072 | tf_op jit(solution)/shard_map/concatenate | solution.py:283
  20.2 0.0 copy-start.1
  20.2 4.0 %collective-permute-start.2 = (bf16[256,128]{1,0:T(8,128)(2,1)S(1)}, bf16[256,128]{1,0:T(8,128)(2,1)S(1)}, u32[]{:S(2)}, u32[]{:S(2)}) collective-permute-start(bf16[256,128]{1,0:T(8,128)(2,1)S(1)} %pad_maximum_fusion.refs_0_), channel_id=1, source_target_pairs={{0,4},{2,6},{4,8},{5,1},{6,10},{7,3},{8,12},{9,5},{10,14},{11,7},{... | collective-permute-start | bytes 196616 | tf_op jit(solution)/shard_map/ppermute | solution.py:285
  24.3 1.9 %collective-permute-start.1 = (bf16[256,128]{1,0:T(8,128)(2,1)S(1)}, bf16[256,128]{1,0:T(8,128)(2,1)S(1)}, u32[]{:S(2)}, u32[]{:S(2)}) collective-permute-start(bf16[256,128]{1,0:T(8,128)(2,1)S(1)} %pad_maximum_fusion.refs_0_), channel_id=1, source_target_pairs={{0,2},{2,4},{3,1},{4,6},{5,3},{6,8},{7,5},{8,10},{9,7},{10,12},{11... | collective-permute-start | bytes 196616 | tf_op jit(solution)/shard_map/ppermute | solution.py:284
  26.2 2.9 %collective-permute-done.2.refs_2_ = bf16[256,128]{1,0:T(8,128)(2,1)S(1)} collective-permute-done((bf16[256,128]{1,0:T(8,128)(2,1)S(1)}, bf16[256,128]{1,0:T(8,128)(2,1)S(1)}, u32[]{:S(2)}, u32[]{:S(2)}) %collective-permute-start.2) | collective-permute-done | bytes 65568 | tf_op jit(solution)/shard_map/ppermute | solution.py:285
  29.1 0.0 copy-start.2
  29.1 1.9 %collective-permute-start.4 = (bf16[256,128]{1,0:T(8,128)(2,1)S(1)}, bf16[256,128]{1,0:T(8,128)(2,1)S(1)}, u32[]{:S(2)}, u32[]{:S(2)}) collective-permute-start(bf16[256,128]{1,0:T(8,128)(2,1)S(1)} %collective-permute-done.2.refs_2_), channel_id=1, source_target_pairs={{0,1},{1,0},{2,3},{3,2},{4,5},{5,4},{6,7},{7,6},{8,9},{9,8},{10,11... | collective-permute-start | bytes 196616 | tf_op jit(solution)/shard_map/ppermute | solution.py:287
  31.0 0.0 collective-permute-done.1.refs_1_
  31.0 0.0 copy-start.3
  31.1 2.4 %collective-permute-start.3 = (bf16[256,128]{1,0:T(8,128)(2,1)S(1)}, bf16[256,128]{1,0:T(8,128)(2,1)S(1)}, u32[]{:S(2)}, u32[]{:S(2)}) collective-permute-start(bf16[256,128]{1,0:T(8,128)(2,1)S(1)} %collective-permute-done.1.refs_1_), channel_id=1, source_target_pairs={{0,1},{1,0},{2,3},{3,2},{4,5},{5,4},{6,7},{7,6},{8,9},{9,8},{10,11... | collective-permute-start | bytes 196616 | tf_op jit(solution)/shard_map/ppermute | solution.py:286
  33.5 0.0 collective-permute-done.4.refs_4_
  33.5 0.0 copy-start.4
  33.5 0.9 %collective-permute-done.3.refs_3_ = bf16[256,128]{1,0:T(8,128)(2,1)S(1)} collective-permute-done((bf16[256,128]{1,0:T(8,128)(2,1)S(1)}, bf16[256,128]{1,0:T(8,128)(2,1)S(1)}, u32[]{:S(2)}, u32[]{:S(2)}) %collective-permute-start.3) | collective-permute-done | bytes 65568 | tf_op jit(solution)/shard_map/ppermute | solution.py:286
  34.3 0.0 copy-start.5
  34.3 4.0 %all-to-all-done = bf16[16,64,128]{2,1,0:T(8,128)(2,1)S(1)} async-done(((bf16[16,64,128]{2,1,0:T(8,128)(2,1)}), bf16[16,64,128]{2,1,0:T(8,128)(2,1)S(1)}, u32[]{:S(2)}, u32[]{:S(2)}) %all-to-all-start) | async-done | bytes 262176 | tf_op jit(solution)/shard_map/all_to_all | solution.py:281
  38.3 0.0 copy-start
  38.3 0.0 copy-done.1
  38.4 0.0 copy-done.2
  38.4 0.0 copy-done.3
  38.4 0.0 copy-done.4
  38.4 0.0 copy-done.5
  38.4 0.7 %copy-done = bf16[16,64,128]{2,1,0:T(8,128)(2,1)} copy-done((bf16[16,64,128]{2,1,0:T(8,128)(2,1)}, bf16[16,64,128]{2,1,0:T(8,128)(2,1)S(1)}, u32[]{:S(2)}) %copy-start) | copy-done | bytes 262168
  39.0 5.0 %correlate.1 = (bf16[64,2048]{1,0:T(8,128)(2,1)}, bf16[2048,128]{1,0:T(8,128)(2,1)}) custom-call(s32[1]{0:T(128)} %bitcast.dev_ref, s32[4,16]{1,0:T(4,128)} %partners_hbm.1, bf16[256,128]{1,0:T(8,128)(2,1)} %copy-done.1, bf16[256,128]{1,0:T(8,128)(2,1)} %copy-done.3, bf16[256,128]{1,0:T(8,128)(2,1)} %copy-done.2, bf16[256,128]{1,0:T(8,128)(2,1)} %copy-done.5, ...), custom_call_target="tpu_custom_call" | custom-call | tf_op jit(solution)/shard_map/correlate/pallas_call | solution.py:290
Async XLA Ops:
  0.6 3.6 %collective-permute-start = (bf16[128,128]{1,0:T(8,128)(2,1)}, bf16[128,128]{1,0:T(8,128)(2,1)S(1)}, u32[]{:S(2)}, u32[]{:S(2)}) collective-permute-start(bf16[128,128]{1,0:T(8,128)(2,1)} %bitcast.17), channel_id=1, source_target_pairs={{0,1},{1,0},{2,3},{3,2},{4,5},{5,4},{6,7},{7,6},{8,9},{9,8},{10,11... | collective-permute-start | bytes 98312 | tf_op jit(solution)/shard_map/ppermute | solution.py:279
  4.3 34.1 %all-to-all-start = ((bf16[16,64,128]{2,1,0:T(8,128)(2,1)}), bf16[16,64,128]{2,1,0:T(8,128)(2,1)S(1)}, u32[]{:S(2)}, u32[]{:S(2)}) async-start(bf16[16,64,128]{2,1,0:T(8,128)(2,1)} %bitcast.16), calls=%async_computation | async-start | bytes 524288 | tf_op jit(solution)/shard_map/all_to_all | solution.py:281
  20.2 18.1 %copy-start.1 = (bf16[256,128]{1,0:T(8,128)(2,1)}, bf16[256,128]{1,0:T(8,128)(2,1)S(1)}, u32[]{:S(2)}) copy-start(bf16[256,128]{1,0:T(8,128)(2,1)S(1)} %pad_maximum_fusion.refs_0_) | copy-start | bytes 196612
  20.2 8.9 %collective-permute-start.2 = (bf16[256,128]{1,0:T(8,128)(2,1)S(1)}, bf16[256,128]{1,0:T(8,128)(2,1)S(1)}, u32[]{:S(2)}, u32[]{:S(2)}) collective-permute-start(bf16[256,128]{1,0:T(8,128)(2,1)S(1)} %pad_maximum_fusion.refs_0_), channel_id=1, source_target_pairs={{0,4},{2,6},{4,8},{5,1},{6,10},{7,3},{8,12},{9,5},{10,14},{11,7},{... | collective-permute-start | bytes 196616 | tf_op jit(solution)/shard_map/ppermute | solution.py:285
  24.3 6.8 %collective-permute-start.1 = (bf16[256,128]{1,0:T(8,128)(2,1)S(1)}, bf16[256,128]{1,0:T(8,128)(2,1)S(1)}, u32[]{:S(2)}, u32[]{:S(2)}) collective-permute-start(bf16[256,128]{1,0:T(8,128)(2,1)S(1)} %pad_maximum_fusion.refs_0_), channel_id=1, source_target_pairs={{0,2},{2,4},{3,1},{4,6},{5,3},{6,8},{7,5},{8,10},{9,7},{10,12},{11... | collective-permute-start | bytes 196616 | tf_op jit(solution)/shard_map/ppermute | solution.py:284
  29.1 9.2 %copy-start.2 = (bf16[256,128]{1,0:T(8,128)(2,1)}, bf16[256,128]{1,0:T(8,128)(2,1)S(1)}, u32[]{:S(2)}) copy-start(bf16[256,128]{1,0:T(8,128)(2,1)S(1)} %collective-permute-done.2.refs_2_) | copy-start | bytes 196612
  29.1 4.4 %collective-permute-start.4 = (bf16[256,128]{1,0:T(8,128)(2,1)S(1)}, bf16[256,128]{1,0:T(8,128)(2,1)S(1)}, u32[]{:S(2)}, u32[]{:S(2)}) collective-permute-start(bf16[256,128]{1,0:T(8,128)(2,1)S(1)} %collective-permute-done.2.refs_2_), channel_id=1, source_target_pairs={{0,1},{1,0},{2,3},{3,2},{4,5},{5,4},{6,7},{7,6},{8,9},{9,8},{10,11... | collective-permute-start | bytes 196616 | tf_op jit(solution)/shard_map/ppermute | solution.py:287
  31.0 7.3 %copy-start.3 = (bf16[256,128]{1,0:T(8,128)(2,1)}, bf16[256,128]{1,0:T(8,128)(2,1)S(1)}, u32[]{:S(2)}) copy-start(bf16[256,128]{1,0:T(8,128)(2,1)S(1)} %collective-permute-done.1.refs_1_) | copy-start | bytes 196612
  31.1 3.3 %collective-permute-start.3 = (bf16[256,128]{1,0:T(8,128)(2,1)S(1)}, bf16[256,128]{1,0:T(8,128)(2,1)S(1)}, u32[]{:S(2)}, u32[]{:S(2)}) collective-permute-start(bf16[256,128]{1,0:T(8,128)(2,1)S(1)} %collective-permute-done.1.refs_1_), channel_id=1, source_target_pairs={{0,1},{1,0},{2,3},{3,2},{4,5},{5,4},{6,7},{7,6},{8,9},{9,8},{10,11... | collective-permute-start | bytes 196616 | tf_op jit(solution)/shard_map/ppermute | solution.py:286
  33.5 4.9 %copy-start.4 = (bf16[256,128]{1,0:T(8,128)(2,1)}, bf16[256,128]{1,0:T(8,128)(2,1)S(1)}, u32[]{:S(2)}) copy-start(bf16[256,128]{1,0:T(8,128)(2,1)S(1)} %collective-permute-done.4.refs_4_) | copy-start | bytes 196612
  34.3 4.0 %copy-start.5 = (bf16[256,128]{1,0:T(8,128)(2,1)}, bf16[256,128]{1,0:T(8,128)(2,1)S(1)}, u32[]{:S(2)}) copy-start(bf16[256,128]{1,0:T(8,128)(2,1)S(1)} %collective-permute-done.3.refs_3_) | copy-start | bytes 196612
  38.3 0.7 %copy-start = (bf16[16,64,128]{2,1,0:T(8,128)(2,1)}, bf16[16,64,128]{2,1,0:T(8,128)(2,1)S(1)}, u32[]{:S(2)}) copy-start(bf16[16,64,128]{2,1,0:T(8,128)(2,1)S(1)} %all-to-all-done) | copy-start | bytes 786436
where the time goes:
time: 44.5 us; the launch traced here: 44 us
  starting transfers between devices  27.4 us (62%)
  waiting for transfers between devices  7.78 us (17%)
  Pallas kernels  6.66 us (15%)
  other arithmetic  0.77 us (2%)
  between operations  0.75 us (2%)
  local copies, waits for them, and re-layouts  0.68 us (2%)
    all_to_all x1, starting transfers between devices, shards(): lax.all_to_all(outgoing.reshape(16, 2 * ROWS, LANES), 'grp', 0, 0, tiled=...  15.2 us
    pallas_call x1, Pallas kernels, shards(): pl.pallas_call(correlate_kernel, out_shape=(like(64, NT), like(64 * FAR,...  4.98 us
    ppermute x1, starting transfers between devices, shards(): two_side = lax.ppermute(chip, 'dev', toward(2))  4.02 us
    all_to_all x1, waiting for transfers between devices, shards(): lax.all_to_all(outgoing.reshape(16, 2 * ROWS, LANES), 'grp', 0, 0, tiled=...  4 us
    ppermute x1, waiting for transfers between devices, shards(): two_side = lax.ppermute(chip, 'dev', toward(2))  2.91 us
    ppermute x1, starting transfers between devices, shards(): one_far = lax.ppermute(one_side, 'dev', swap)  2.41 us
    ppermute x1, starting transfers between devices, shards(): other = lax.ppermute(raw, 'dev', swap)  1.92 us
    ppermute x1, starting transfers between devices, shards(): one_side = lax.ppermute(chip, 'dev', toward(1))  1.92 us
  transfers between devices with their start and end apart: 6, of which 3 were waited for; matrix products, arithmetic and copies ran while one was open for 2% of the time, Pallas kernels for 4%

commit v1 on v0

--- a/solution.py
+++ b/solution.py
@@ -19,24 +19,13 @@
 
 def make_tables():
     b = np.arange(256)
-    k = np.arange(128)
-
-    def trig(bins):
-        angle = (b[:, None] * bins[None, :]) % NT * (2.0 * np.pi / NT)
-        return np.cos(angle), np.sin(angle)
-
-    tiles = [np.concatenate([cos, -sin], axis=1) for cos, sin in (trig(8 * k), trig(8 * k + 4))]
-    for r in (2, 1, 3):
-        tiles += trig(np.concatenate([8 * k + r, -(8 * k + 8 - r)]))
-
-    def stacked(tiles):
-        cut = [tile[:, lo : lo + LANES] for tile in tiles for lo in (0, LANES)]
-        return np.concatenate(cut, axis=0).astype(np.float32).astype(jnp.bfloat16)
-
-    return stacked(tiles + [tile.T for tile in tiles])
-
-
-TILES = 8
+    angle = b[:, None] * b[None, :] % 256 * (2.0 * np.pi / 256)
+    blocks = [f(angle)[:, lo : lo + LANES] for f in (np.cos, np.sin) for lo in (0, LANES)]
+    turn = np.array([2, 1, 3, 4])[:, None] * b[None, :] * (2.0 * np.pi / NT)
+    twiddles = np.concatenate([np.cos(turn), np.sin(turn)], axis=0).astype(np.float32)
+    return np.concatenate(blocks, axis=0).astype(np.float32).astype(jnp.bfloat16), twiddles
+
+
 VMEM_LIMIT = 60 * 1024 * 1024
 
 
@@ -51,20 +40,21 @@
     return moves
 
 
-def tile(table_ref, m):
-    return jnp.concatenate([table_ref[pl.ds(512 * m, 256), :], table_ref[pl.ds(512 * m + 256, 256), :]], axis=1)
-
-
-def products(one_ref, two_ref, y_ref, n, table_ref, first, sign):
-    for m in range(2):
-        y_ref[0:n, 256 * m : 256 * (m + 1)] = dot(one_ref[m], tile(table_ref, first + m))
-    for m in range(3):
-        c = dot(two_ref[m], tile(table_ref, first + 2 + 2 * m))
-        s = dot(two_ref[m], tile(table_ref, first + 3 + 2 * m))
-        col = 512 * (m + 1)
-        re, im = (c[:n] + s[n:], c[n:] - s[:n]) if sign == 1 else (c[:n] - s[n:], c[n:] + s[:n])
-        y_ref[0:n, col : col + 256] = re
-        y_ref[0:n, col + 256 : col + 512] = im
+def whole(table_ref):
+    c0, c1, s0, s1 = (table_ref[pl.ds(256 * m, 256), :] for m in range(4))
+    top = jnp.concatenate([c0, c1, -s0, -s1], axis=1)
+    return jnp.concatenate([top, jnp.concatenate([s0, s1, c0, c1], axis=1)], axis=0)
+
+
+def half(table_ref):
+    c, s = table_ref[pl.ds(0, 256), :], table_ref[pl.ds(512, 256), :]
+    return jnp.concatenate([jnp.concatenate([c, -s], axis=1), jnp.concatenate([s, c], axis=1)], axis=0)
+
+
+def half_inverse(table_ref):
+    c0, c1, s0, s1 = (table_ref[pl.ds(256 * m, LANES), :] for m in range(4))
+    top = jnp.concatenate([c0, c1, -s0, -s1], axis=1)
+    return jnp.concatenate([top, jnp.concatenate([s0, s1, c0, c1], axis=1)], axis=0)
 
 
 def select_kernel(routes_hbm, own_hbm, out_ref, routes_ref, own_ref, sems):
@@ -85,30 +75,59 @@
         x_ref[pl.ds((start + c) * stride, ROWS), :] = blk_ref[pl.ds(c * ROWS, ROWS), :].astype(F32)
 
 
-def forward(x_ref, stride, n, one_ref, two_ref, z_ref, table_ref, move):
-    for w in range(2):
-        for half in range(2):
-            x = [x_ref[pl.ds(2 * (2 * a + half) + w, n, stride=stride), :] for a in range(8)]
+def forward(x_ref, stride, n, one_ref, four_ref, two_ref, z_ref, table_ref, tw_ref, moves):
+    rows = 2 * n
+    moves[1].wait()
+    for part in range(2):
+        lanes = pl.ds(part * LANES, LANES)
+        lanes_im = pl.ds(256 + part * LANES, LANES)
+        cos = [jnp.broadcast_to(tw_ref[m : m + 1, lanes], (n, LANES)) for m in range(4)]
+        sin = [jnp.broadcast_to(tw_ref[m + 4 : m + 5, lanes], (n, LANES)) for m in range(4)]
+        for w in range(2):
+            x = [x_ref[pl.ds(2 * (2 * a + part) + w, n, stride=stride), :] for a in range(8)]
             s = [x[a] + x[a + 4] for a in range(4)]
             d = [x[a] - x[a + 4] for a in range(4)]
             even, odd = s[0] + s[2], s[1] + s[3]
             diff, summ = C * (d[1] - d[3]), C * (d[1] + d[3])
-            lanes = pl.ds(half * LANES, LANES)
-            for m, part in enumerate((even + odd, even - odd)):
-                one_ref[m, pl.ds(w * n, n), lanes] = part.astype(BF16)
-            for m, parts in enumerate(
+            one_ref[pl.ds(w * n, n), lanes] = (even + odd).astype(BF16)
+            four = even - odd
+            four_ref[pl.ds(w * n, n), lanes] = (four * cos[3]).astype(BF16)
+            four_ref[pl.ds(w * n, n), lanes_im] = (-four * sin[3]).astype(BF16)
+            for m, (re, im) in enumerate(
                 ((s[0] - s[2], s[3] - s[1]), (d[0] + diff, -d[2] - summ), (d[0] - diff, d[2] - summ))
             ):
-                for k, part in enumerate(parts):
-                    two_ref[m, pl.ds((2 * k + w) * n, n), lanes] = part.astype(BF16)
-    move.wait()
-    products(one_ref, two_ref, z_ref, 2 * n, table_ref, 0, 1)
+                two_ref[pl.ds(m * rows + w * n, n), lanes] = (re * cos[m] + im * sin[m]).astype(BF16)
+                two_ref[pl.ds(m * rows + w * n, n), lanes_im] = (im * cos[m] - re * sin[m]).astype(BF16)
+    moves[0].wait()
+    table = half(table_ref)
+    z_ref[:, 0:256] = dot(one_ref[...], table[0:256])
+    z_ref[:, 256:512] = dot(four_ref[...], table)
+    table = whole(table_ref)
+    y = dot(two_ref[...], table)
+    for m in range(3):
+        z_ref[:, 512 * (m + 1) : 512 * (m + 2)] = y[m * rows : (m + 1) * rows]
     total = None
     for re, im in COLS:
-        zr, zi = z_ref[0 : 2 * n, re : re + LANES], z_ref[0 : 2 * n, im : im + LANES]
+        zr, zi = z_ref[:, re : re + LANES], z_ref[:, im : im + LANES]
         energy = zr * zr + zi * zi
         total = energy if total is None else total + energy
     return jnp.sum(total, axis=1, keepdims=True) * (1.0 / BINS)
+
+
+def backward(one_ref, two_ref, h_ref, n, table_ref, tw_ref):
+    table = half_inverse(table_ref)
+    h_ref[:, 0:256] = dot(one_ref[pl.ds(0, n), :], table[:, 0:256])
+    y = dot(one_ref[pl.ds(n, n), :], table)
+    h_ref[:, 256:512] = y[:, 0:256] * tw_ref[3:4, :] + y[:, 256:512] * tw_ref[7:8, :]
+    table = whole(table_ref)
+    whole_y = dot(two_ref[...], table)
+    for m in range(3):
+        y = whole_y[m * n : (m + 1) * n]
+        re, minus_im = y[:, 0:256], y[:, 256:512]
+        cos, sin = tw_ref[m : m + 1, :], tw_ref[m + 4 : m + 5, :]
+        col = 512 * (m + 1)
+        h_ref[:, col : col + 256] = re * cos + minus_im * sin
+        h_ref[:, col + 256 : col + 512] = re * sin - minus_im * cos
 
 
 def whitened(z_ref, level, re, im):
@@ -122,13 +141,14 @@
     n = sr.shape[0]
     sr, si = (sr * (1.0 / 64)).astype(BF16), (si * (1.0 / 64)).astype(BF16)
     if chunk < 2:
-        one_ref[chunk, pl.ds(lo, n), 0:LANES] = sr
-        one_ref[chunk, pl.ds(lo, n), LANES : 2 * LANES] = si
+        rows = pl.ds(chunk * (one_ref.shape[0] // 2) + lo, n)
+        one_ref[rows, 0:LANES] = sr
+        one_ref[rows, LANES : 2 * LANES] = -si
     else:
-        rows = two_ref.shape[1] // 2
-        m, lanes = (chunk - 2) // 2, pl.ds(chunk % 2 * LANES, LANES)
-        two_ref[m, pl.ds(lo, n), lanes] = sr
-        two_ref[m, pl.ds(rows + lo, n), lanes] = si
+        rows = pl.ds((chunk - 2) // 2 * (two_ref.shape[0] // 3) + lo, n)
+        at = chunk % 2 * LANES
+        two_ref[rows, at : at + LANES] = sr
+        two_ref[rows, 256 + at : 256 + at + LANES] = -si
 
 
 def lags(h_ref, lo, n, half):
@@ -167,27 +187,19 @@
 
 
 def correlate_kernel(dev_ref, partners_hbm, *refs):
-    near_hbm, (recv_hbm, table_hbm, near_out, far_out), refs = refs[:5], refs[5:9], refs[9:]
-    near_refs, (recv_ref, table_ref, partners_ref), refs = refs[:5], refs[5:8], refs[8:]
-    x_ref, u1_ref, u2_ref, z_ref, w_ref, p_ref, s1_ref, s2_ref, h_ref, o_ref, near_ref, far_ref, sems, out_sems = refs
-    half = 512 * TILES
-    moves = fetch(
-        [
-            (table_hbm.at[pl.ds(0, half), :], table_ref.at[pl.ds(0, half), :]),
-            *zip(near_hbm, near_refs),
-            (recv_hbm, recv_ref),
-            (partners_hbm, partners_ref),
-            (table_hbm.at[pl.ds(half, half), :], table_ref.at[pl.ds(half, half), :]),
-        ],
-        sems,
-    )
+    near_hbm, (recv_hbm, table_hbm, tw_hbm, near_out, far_out), refs = refs[:3], refs[3:8], refs[8:]
+    near_refs, (recv_ref, table_ref, tw_ref, partners_ref), refs = refs[:3], refs[3:7], refs[7:]
+    x_ref, u1_ref, u4_ref, u2_ref, z_ref, w_ref, p_ref, s1_ref, s2_ref, h_ref, o_ref, near_ref, far_ref, sems, out_sems = refs
+    inputs = [*zip(near_hbm, near_refs), (recv_hbm, recv_ref)]
+    moves = fetch([*inputs, (tw_hbm, tw_ref), (table_hbm, table_ref), (partners_hbm, partners_ref)], sems)
     x_ref[pl.ds(40 * STRIDE, 8 * STRIDE), :] = jnp.zeros((8 * STRIDE, LANES), F32)
-    for move in moves[1:8]:
+    start = 0
+    for move, ref in zip(moves, (*near_refs, recv_ref)):
         move.wait()
-    for m, ref in enumerate(near_refs):
-        spread(x_ref, STRIDE, 8 * m, ref, 8)
-    spread(x_ref, STRIDE, NEAR, recv_ref, FAR)
-    level = 0.1 * forward(x_ref, STRIDE, N, u1_ref, u2_ref, z_ref, table_ref, moves[0]) + 1e-6
+        start = NEAR if ref is recv_ref else start
+        spread(x_ref, STRIDE, start, ref, ref.shape[0] // ROWS)
+        start += ref.shape[0] // ROWS
+    level = 0.1 * forward(x_ref, STRIDE, N, u1_ref, u4_ref, u2_ref, z_ref, table_ref, tw_ref, (moves[5], moves[4])) + 1e-6
     for chunk, (re, im) in enumerate(COLS):
         wr, wi = whitened(z_ref, level, re, im)
         for w in range(2):
@@ -202,6 +214,7 @@
                 sr = sr + (fr * br + fi * bi)
                 si = si + (fi * br - fr * bi)
             put(s1_ref, s2_ref, chunk, 64 + i * FAR, sr, si)
+    moves[6].wait()
     picker = picked(dev_ref[0], partners_ref)
     for w in range(2):
         p_ref[w] = dot(picker, w_ref[w])
@@ -215,8 +228,7 @@
                 sr = sr + (ar * pr + ai * pi)
                 si = si + (ai * pr - ar * pi)
             put(s1_ref, s2_ref, chunk, c * 16, sr, si)
-    moves[8].wait()
-    products(s1_ref, s2_ref, h_ref, PAIRS, table_ref, TILES, -1)
+    backward(s1_ref, s2_ref, h_ref, PAIRS, table_ref, tw_ref)
     for lo in range(0, 64, 16):
         for part in range(2):
             for a, lag in enumerate(lags(h_ref, lo, 16, part)):
@@ -255,7 +267,7 @@
 
 
 def shards(records, partners, routes):
-    table = jnp.asarray(make_tables())
+    table, twiddles = (jnp.asarray(x) for x in make_tables())
     members = lax.axis_size("dev")
     swap = [(d, d ^ 1) for d in range(members)]
 
@@ -277,42 +289,43 @@
         name="select",
     )(routes.T, raw)
     other = lax.ppermute(raw, "dev", swap)
-    outgoing, other = lax.optimization_barrier((outgoing, other))
     arrived = lax.all_to_all(outgoing.reshape(16, 2 * ROWS, LANES), "grp", 0, 0, tiled=True).reshape(32 * ROWS, LANES)
 
     chip = jnp.concatenate([raw, other], axis=0)
     one_side = lax.ppermute(chip, "dev", toward(1))
     two_side = lax.ppermute(chip, "dev", toward(2))
-    one_far = lax.ppermute(one_side, "dev", swap)
-    two_far = lax.ppermute(two_side, "dev", swap)
+    side = jnp.concatenate([one_side, two_side], axis=0)
+    far_side = lax.ppermute(side, "dev", swap)
     dev = lax.axis_index("dev").astype(jnp.int32).reshape(1)
-    blocks = (chip, one_side, two_side, one_far, two_far)
+    blocks = (chip, side, far_side)
     near, far = pl.pallas_call(
         correlate_kernel,
         out_shape=(like(64, NT), like(64 * FAR, LANES)),
-        in_specs=[smem()] + [hbm()] * 8,
+        in_specs=[smem()] + [hbm()] * 7,
         out_specs=(hbm(), hbm()),
         scratch_shapes=[pltpu.VMEM(x.shape, BF16) for x in (*blocks, arrived, table)]
         + [
+            pltpu.VMEM(twiddles.shape, F32),
             pltpu.SMEM((4, 16), jnp.int32),
             pltpu.VMEM((N * STRIDE, LANES), F32),
-            pltpu.VMEM((2, 2 * N, 256), BF16),
-            pltpu.VMEM((3, 4 * N, 256), BF16),
+            pltpu.VMEM((2 * N, 256), BF16),
+            pltpu.VMEM((2 * N, 512), BF16),
+            pltpu.VMEM((6 * N, 512), BF16),
             pltpu.VMEM((2 * N, NT), F32),
             pltpu.VMEM((2, NEAR, NT), BF16),
             pltpu.VMEM((2, 64, NT), F32),
-            pltpu.VMEM((2, PAIRS, 256), BF16),
-            pltpu.VMEM((3, 2 * PAIRS, 256), BF16),
+            pltpu.VMEM((2 * PAIRS, 256), BF16),
+            pltpu.VMEM((3 * PAIRS, 512), BF16),
             pltpu.VMEM((PAIRS, NT), F32),
             pltpu.VMEM((FAR * SLOT, LANES), F32),
             pltpu.VMEM((64, NT), BF16),
             pltpu.VMEM((64 * FAR, LANES), BF16),
-            pltpu.SemaphoreType.DMA((9,)),
+            pltpu.SemaphoreType.DMA((7,)),
             pltpu.SemaphoreType.DMA((1 + FAR // GROUP,)),
         ],
         compiler_params=pltpu.CompilerParams(vmem_limit_bytes=VMEM_LIMIT),
         name="correlate",
-    )(dev, partners, *blocks, arrived, table)
+    )(dev, partners, *blocks, arrived, table, twiddles)
     far = far.reshape(32, 16, 4, LANES).transpose(0, 2, 1, 3).reshape(1, 1, 32, 4, NT)
     return (near.reshape(4, 16, NT), far)
 

time: 44.5 us -> 42.1 us (0.946)
  the two profiles are of different devices: /device:TPU:26 before, /device:TPU:57 now
where the time goes in v1:
time: 42.1 us; the launch traced here: 41.7 us
  starting transfers between devices  27.7 us (66%)
  Pallas kernels  6.38 us (15%)
  waiting for transfers between devices  6.14 us (15%)
  local copies, waits for them, and re-layouts  0.78 us (2%)
  between operations  0.72 us (2%)
    all_to_all x1, starting transfers between devices, shards(): lax.all_to_all(outgoing.reshape(16, 2 * ROWS, LANES), 'grp', 0, 0, tiled=...  14.7 us
    pallas_call x1, Pallas kernels, shards(): pl.pallas_call(correlate_kernel, out_shape=(like(64, NT), like(64 * FAR,...  4.7 us
    ppermute x1, starting transfers between devices, shards(): one_side = lax.ppermute(chip, 'dev', toward(1))  4.55 us
    ppermute x1, waiting for transfers between devices, shards(): two_side = lax.ppermute(chip, 'dev', toward(2))  4.34 us
    ppermute x1, starting transfers between devices, shards(): other = lax.ppermute(raw, 'dev', swap)  3.14 us
    ppermute x1, starting transfers between devices, shards(): far_side = lax.ppermute(side, 'dev', swap)  2.89 us
    ppermute x1, starting transfers between devices, shards(): two_side = lax.ppermute(chip, 'dev', toward(2))  2.43 us
    pallas_call x1, Pallas kernels, shards(): pl.pallas_call(select_kernel, out_shape=like(32 * ROWS, LANES), in_specs=...  1.68 us
  transfers between devices with their start and end apart: 5, of which 3 were waited for; matrix products, arithmetic and copies ran while one was open for 0% of the time, Pallas kernels for 0%

profile of v1, /device:TPU:57, one launch (start us, length us, event | category | flops | bytes accessed | tf_op | source)
XLA Modules:
  0.0 41.7 jit_solution(12415771502055621498)
XLA Ops:
  0.6 1.7 %select.1 = bf16[1024,128]{1,0:T(8,128)(2,1)} custom-call(s32[2,4]{1,0:T(2,128)} %bitcast.20, bf16[128,128]{1,0:T(8,128)(2,1)} %bitcast.17), custom_call_target="tpu_custom_call" | custom-call | tf_op jit(solution)/shard_map/select/pallas_call | solution.py:279
  2.3 0.0 copy-start.3
  2.3 14.7 %all-to-all-start = ((bf16[16,64,128]{2,1,0:T(8,128)(2,1)}), bf16[16,64,128]{2,1,0:T(8,128)(2,1)S(1)}, u32[]{:S(2)}, u32[]{:S(2)}) async-start(bf16[16,64,128]{2,1,0:T(8,128)(2,1)} %bitcast.16), calls=%async_computation | async-start | bytes 524288 | tf_op jit(solution)/shard_map/all_to_all | solution.py:292
  17.0 0.0 copy-done.3
  17.0 3.1 %collective-permute-start = (bf16[128,128]{1,0:T(8,128)(2,1)S(1)}, bf16[128,128]{1,0:T(8,128)(2,1)S(1)}, u32[]{:S(2)}, u32[]{:S(2)}) collective-permute-start(bf16[128,128]{1,0:T(8,128)(2,1)S(1)} %bitcast.18), channel_id=1, source_target_pairs={{0,1},{1,0},{2,3},{3,2},{4,5},{5,4},{6,7},{7,6},{8,9},{9,8},{10,11... | collective-permute-start | bytes 98312 | tf_op jit(solution)/shard_map/ppermute | solution.py:291
  20.1 0.8 %collective-permute-done = bf16[128,128]{1,0:T(8,128)(2,1)S(1)} collective-permute-done((bf16[128,128]{1,0:T(8,128)(2,1)S(1)}, bf16[128,128]{1,0:T(8,128)(2,1)S(1)}, u32[]{:S(2)}, u32[]{:S(2)}) %collective-permute-start) | collective-permute-done | bytes 32800 | tf_op jit(solution)/shard_map/ppermute | solution.py:291
  21.0 0.0 copy-start.2
  21.0 4.6 %collective-permute-start.1 = (bf16[256,128]{1,0:T(8,128)(2,1)S(1)}, bf16[256,128]{1,0:T(8,128)(2,1)S(1)}, u32[]{:S(2)}, u32[]{:S(2)}) collective-permute-start(bf16[256,128]{1,0:T(8,128)(2,1)S(1)} %pad_maximum_fusion.refs_0_), channel_id=1, source_target_pairs={{0,2},{2,4},{3,1},{4,6},{5,3},{6,8},{7,5},{8,10},{9,7},{10,12},{11... | collective-permute-start | bytes 196616 | tf_op jit(solution)/shard_map/ppermute | solution.py:295
  25.6 2.4 %collective-permute-start.2 = (bf16[256,128]{1,0:T(8,128)(2,1)S(1)}, bf16[256,128]{1,0:T(8,128)(2,1)S(1)}, u32[]{:S(2)}, u32[]{:S(2)}) collective-permute-start(bf16[256,128]{1,0:T(8,128)(2,1)S(1)} %pad_maximum_fusion.refs_0_), channel_id=1, source_target_pairs={{0,4},{2,6},{4,8},{5,1},{6,10},{7,3},{8,12},{9,5},{10,14},{11,7},{... | collective-permute-start | bytes 196616 | tf_op jit(solution)/shard_map/ppermute | solution.py:296
  28.0 0.0 collective-permute-done.1
  28.0 0.0 copy-done.2
  28.0 4.3 %collective-permute-done.2 = bf16[256,128]{1,0:T(8,128)(2,1)S(1)} collective-permute-done((bf16[256,128]{1,0:T(8,128)(2,1)S(1)}, bf16[256,128]{1,0:T(8,128)(2,1)S(1)}, u32[]{:S(2)}, u32[]{:S(2)}) %collective-permute-start.2) | collective-permute-done | bytes 65568 | tf_op jit(solution)/shard_map/ppermute | solution.py:296
  32.4 0.0 copy-start.1
  32.4 2.9 %collective-permute-start.3 = (bf16[512,128]{1,0:T(8,128)(2,1)S(1)}, bf16[512,128]{1,0:T(8,128)(2,1)S(1)}, u32[]{:S(2)}, u32[]{:S(2)}) collective-permute-start(bf16[512,128]{1,0:T(8,128)(2,1)S(1)} %constant_dynamic-update-slice_fusion.refs_1_), channel_id=1, source_target_pairs={{0,1},{1,0},{2,3},{3,2},{4,5},{5,4},{6,7},{7,6},{8,9},{9,8},{10,11... | collective-permute-start | bytes 393224 | tf_op jit(solution)/shard_map/ppermute | solution.py:298
  35.3 1.0 %collective-permute-done.3.refs_2_ = bf16[512,128]{1,0:T(8,128)(2,1)S(1)} collective-permute-done((bf16[512,128]{1,0:T(8,128)(2,1)S(1)}, bf16[512,128]{1,0:T(8,128)(2,1)S(1)}, u32[]{:S(2)}, u32[]{:S(2)}) %collective-permute-start.3) | collective-permute-done | bytes 131104 | tf_op jit(solution)/shard_map/ppermute | solution.py:298
  36.3 0.0 copy-start.4
  36.3 0.0 all-to-all-done
  36.3 0.0 copy-start
  36.3 0.0 copy-done.1
  36.3 0.6 %copy-done.4 = bf16[512,128]{1,0:T(8,128)(2,1)} copy-done((bf16[512,128]{1,0:T(8,128)(2,1)}, bf16[512,128]{1,0:T(8,128)(2,1)S(1)}, u32[]{:S(2)}) %copy-start.4) | copy-done | bytes 131096
  36.9 0.1 copy-done
  37.0 4.7 %correlate.1 = (bf16[64,2048]{1,0:T(8,128)(2,1)}, bf16[2048,128]{1,0:T(8,128)(2,1)}) custom-call(s32[1]{0:T(128)} %bitcast.dev_ref, s32[4,16]{1,0:T(4,128)} %partners_hbm.1, bf16[256,128]{1,0:T(8,128)(2,1)} %copy-done.2, bf16[512,128]{1,0:T(8,128)(2,1)} %copy-done.1, bf16[512,128]{1,0:T(8,128)(2,1)} %copy-done.4, bf16[1024,128]{1,0:T(8,128)(2,1)} %bitcast.15, ...), custom_call_target="tpu_custom_call" | custom-call | tf_op jit(solution)/shard_map/correlate/pallas_call | solution.py:301
  (3 shorter events, 0.0 us)
Async XLA Ops:
  2.3 14.7 %copy-start.3 = (bf16[4,2,2048]{2,1,0:T(2,128)(2,1)S(1)}, bf16[4,2,2048]{2,1,0:T(2,128)(2,1)}, u32[]{:S(2)}) copy-start(bf16[4,2,2048]{2,1,0:T(2,128)(2,1)} %param.5) | copy-start | bytes 98308
  2.3 33.9 %all-to-all-start = ((bf16[16,64,128]{2,1,0:T(8,128)(2,1)}), bf16[16,64,128]{2,1,0:T(8,128)(2,1)S(1)}, u32[]{:S(2)}, u32[]{:S(2)}) async-start(bf16[16,64,128]{2,1,0:T(8,128)(2,1)} %bitcast.16), calls=%async_computation | async-start | bytes 524288 | tf_op jit(solution)/shard_map/all_to_all | solution.py:292
  17.0 4.0 %collective-permute-start = (bf16[128,128]{1,0:T(8,128)(2,1)S(1)}, bf16[128,128]{1,0:T(8,128)(2,1)S(1)}, u32[]{:S(2)}, u32[]{:S(2)}) collective-permute-start(bf16[128,128]{1,0:T(8,128)(2,1)S(1)} %bitcast.18), channel_id=1, source_target_pairs={{0,1},{1,0},{2,3},{3,2},{4,5},{5,4},{6,7},{7,6},{8,9},{9,8},{10,11... | collective-permute-start | bytes 98312 | tf_op jit(solution)/shard_map/ppermute | solution.py:291
  21.0 7.0 %copy-start.2 = (bf16[256,128]{1,0:T(8,128)(2,1)}, bf16[256,128]{1,0:T(8,128)(2,1)S(1)}, u32[]{:S(2)}) copy-start(bf16[256,128]{1,0:T(8,128)(2,1)S(1)} %pad_maximum_fusion.refs_0_) | copy-start | bytes 196612
  21.0 7.0 %collective-permute-start.1 = (bf16[256,128]{1,0:T(8,128)(2,1)S(1)}, bf16[256,128]{1,0:T(8,128)(2,1)S(1)}, u32[]{:S(2)}, u32[]{:S(2)}) collective-permute-start(bf16[256,128]{1,0:T(8,128)(2,1)S(1)} %pad_maximum_fusion.refs_0_), channel_id=1, source_target_pairs={{0,2},{2,4},{3,1},{4,6},{5,3},{6,8},{7,5},{8,10},{9,7},{10,12},{11... | collective-permute-start | bytes 196616 | tf_op jit(solution)/shard_map/ppermute | solution.py:295
  25.6 6.8 %collective-permute-start.2 = (bf16[256,128]{1,0:T(8,128)(2,1)S(1)}, bf16[256,128]{1,0:T(8,128)(2,1)S(1)}, u32[]{:S(2)}, u32[]{:S(2)}) collective-permute-start(bf16[256,128]{1,0:T(8,128)(2,1)S(1)} %pad_maximum_fusion.refs_0_), channel_id=1, source_target_pairs={{0,4},{2,6},{4,8},{5,1},{6,10},{7,3},{8,12},{9,5},{10,14},{11,7},{... | collective-permute-start | bytes 196616 | tf_op jit(solution)/shard_map/ppermute | solution.py:296
  32.4 3.9 %copy-start.1 = (bf16[512,128]{1,0:T(8,128)(2,1)}, bf16[512,128]{1,0:T(8,128)(2,1)S(1)}, u32[]{:S(2)}) copy-start(bf16[512,128]{1,0:T(8,128)(2,1)S(1)} %constant_dynamic-update-slice_fusion.refs_1_) | copy-start | bytes 393220
  32.4 3.9 %collective-permute-start.3 = (bf16[512,128]{1,0:T(8,128)(2,1)S(1)}, bf16[512,128]{1,0:T(8,128)(2,1)S(1)}, u32[]{:S(2)}, u32[]{:S(2)}) collective-permute-start(bf16[512,128]{1,0:T(8,128)(2,1)S(1)} %constant_dynamic-update-slice_fusion.refs_1_), channel_id=1, source_target_pairs={{0,1},{1,0},{2,3},{3,2},{4,5},{5,4},{6,7},{7,6},{8,9},{9,8},{10,11... | collective-permute-start | bytes 393224 | tf_op jit(solution)/shard_map/ppermute | solution.py:298
  36.3 0.6 %copy-start.4 = (bf16[512,128]{1,0:T(8,128)(2,1)}, bf16[512,128]{1,0:T(8,128)(2,1)S(1)}, u32[]{:S(2)}) copy-start(bf16[512,128]{1,0:T(8,128)(2,1)S(1)} %collective-permute-done.3.refs_2_) | copy-start | bytes 393220
  36.3 0.7 %copy-start = (bf16[16,64,128]{2,1,0:T(8,128)(2,1)}, bf16[16,64,128]{2,1,0:T(8,128)(2,1)S(1)}, u32[]{:S(2)}) copy-start(bf16[16,64,128]{2,1,0:T(8,128)(2,1)S(1)} %all-to-all-done) | copy-start | bytes 786436

commit v2 on v1

--- a/solution.py
+++ b/solution.py
@@ -13,17 +13,24 @@
 LANES = 128
 ROWS = 32
 C = math.sqrt(0.5)
-COLS = ((0, 128), (256, 384), (512, 768), (640, 896), (1024, 1280), (1152, 1408), (1536, 1792), (1664, 1920))
+TURN = [(math.cos(math.pi * r / 8), math.sin(math.pi * r / 8)) for r in range(4)]
+COLS = tuple((256 * m, 256 * m + 128) for m in range(8))
 F32, BF16 = jnp.float32, jnp.bfloat16
 
 
 def make_tables():
-    b = np.arange(256)
-    angle = b[:, None] * b[None, :] % 256 * (2.0 * np.pi / 256)
-    blocks = [f(angle)[:, lo : lo + LANES] for f in (np.cos, np.sin) for lo in (0, LANES)]
-    turn = np.array([2, 1, 3, 4])[:, None] * b[None, :] * (2.0 * np.pi / NT)
+    b = np.arange(LANES)
+    angle = b[:, None] * b[None, :] % LANES * (2.0 * np.pi / LANES)
+    c, s = np.cos(angle), np.sin(angle)
+    whole = np.block([[c, -s], [s, c]])
+    c, s = c[:, :64], s[:, :64]
+    o = np.zeros_like(c)
+    ends = np.block([[c, o, -s, o], [o, c, o, -s], [o, s, o, c]])
+    turn = np.arange(1, 9)[:, None] * b[None, :] * (2.0 * np.pi / NT)
     twiddles = np.concatenate([np.cos(turn), np.sin(turn)], axis=0).astype(np.float32)
-    return np.concatenate(blocks, axis=0).astype(np.float32).astype(jnp.bfloat16), twiddles
+    table = np.concatenate([whole, ends], axis=0)
+    table = np.concatenate([table[:, :LANES], table[:, LANES:]], axis=0)
+    return table.astype(np.float32).astype(jnp.bfloat16), twiddles
 
 
 VMEM_LIMIT = 60 * 1024 * 1024
@@ -40,21 +47,23 @@
     return moves
 
 
-def whole(table_ref):
-    c0, c1, s0, s1 = (table_ref[pl.ds(256 * m, 256), :] for m in range(4))
-    top = jnp.concatenate([c0, c1, -s0, -s1], axis=1)
-    return jnp.concatenate([top, jnp.concatenate([s0, s1, c0, c1], axis=1)], axis=0)
-
-
-def half(table_ref):
-    c, s = table_ref[pl.ds(0, 256), :], table_ref[pl.ds(512, 256), :]
-    return jnp.concatenate([jnp.concatenate([c, -s], axis=1), jnp.concatenate([s, c], axis=1)], axis=0)
-
-
-def half_inverse(table_ref):
-    c0, c1, s0, s1 = (table_ref[pl.ds(256 * m, LANES), :] for m in range(4))
-    top = jnp.concatenate([c0, c1, -s0, -s1], axis=1)
-    return jnp.concatenate([top, jnp.concatenate([s0, s1, c0, c1], axis=1)], axis=0)
+def dot_t(a, b):
+    return lax.dot_general(a, b, (((1,), (1,)), ((), ())), preferred_element_type=F32)
+
+
+def tables(table_ref):
+    side = table_ref.shape[0] // 2
+    whole = jnp.concatenate([table_ref[0:256, :], table_ref[side : side + 256, :]], axis=1)
+    ends = jnp.concatenate([table_ref[256:side, :], table_ref[side + 256 : 2 * side, :]], axis=1)
+    return whole, ends
+
+
+def eight(x):
+    s = [x[a] + x[a + 4] for a in range(4)]
+    d = [x[a] - x[a + 4] for a in range(4)]
+    even, odd = s[0] + s[2], s[1] + s[3]
+    diff, summ = C * (d[1] - d[3]), C * (d[1] + d[3])
+    return even + odd, even - odd, ((d[0] + diff, -d[2] - summ), (s[0] - s[2], s[3] - s[1]), (d[0] - diff, d[2] - summ))
 
 
 def select_kernel(routes_hbm, own_hbm, out_ref, routes_ref, own_ref, sems):
@@ -75,37 +84,37 @@
         x_ref[pl.ds((start + c) * stride, ROWS), :] = blk_ref[pl.ds(c * ROWS, ROWS), :].astype(F32)
 
 
-def forward(x_ref, stride, n, one_ref, four_ref, two_ref, z_ref, table_ref, tw_ref, moves):
+def forward(x_ref, stride, n, one_ref, two_ref, z_ref, table_ref, tw_ref, moves):
     rows = 2 * n
     moves[1].wait()
-    for part in range(2):
-        lanes = pl.ds(part * LANES, LANES)
-        lanes_im = pl.ds(256 + part * LANES, LANES)
-        cos = [jnp.broadcast_to(tw_ref[m : m + 1, lanes], (n, LANES)) for m in range(4)]
-        sin = [jnp.broadcast_to(tw_ref[m + 4 : m + 5, lanes], (n, LANES)) for m in range(4)]
-        for w in range(2):
-            x = [x_ref[pl.ds(2 * (2 * a + part) + w, n, stride=stride), :] for a in range(8)]
-            s = [x[a] + x[a + 4] for a in range(4)]
-            d = [x[a] - x[a + 4] for a in range(4)]
-            even, odd = s[0] + s[2], s[1] + s[3]
-            diff, summ = C * (d[1] - d[3]), C * (d[1] + d[3])
-            one_ref[pl.ds(w * n, n), lanes] = (even + odd).astype(BF16)
-            four = even - odd
-            four_ref[pl.ds(w * n, n), lanes] = (four * cos[3]).astype(BF16)
-            four_ref[pl.ds(w * n, n), lanes_im] = (-four * sin[3]).astype(BF16)
-            for m, (re, im) in enumerate(
-                ((s[0] - s[2], s[3] - s[1]), (d[0] + diff, -d[2] - summ), (d[0] - diff, d[2] - summ))
-            ):
-                two_ref[pl.ds(m * rows + w * n, n), lanes] = (re * cos[m] + im * sin[m]).astype(BF16)
-                two_ref[pl.ds(m * rows + w * n, n), lanes_im] = (im * cos[m] - re * sin[m]).astype(BF16)
+    cos = [jnp.broadcast_to(tw_ref[m : m + 1, :], (16, LANES)) for m in range(8)]
+    sin = [jnp.broadcast_to(tw_ref[m + 8 : m + 9, :], (16, LANES)) for m in range(8)]
+    for w in range(2):
+        for lo in range(0, n, 16):
+            x = [x_ref[pl.ds(lo * stride + 2 * a + w, 16, stride=stride), :] for a in range(16)]
+            e0, e4, e = eight(x[0::2])
+            o0, o4, o = eight(x[1::2])
+            at = pl.ds(w * n + lo, 16)
+            last = e0 - o0
+            one_ref[at, 0:128] = (e0 + o0).astype(BF16)
+            one_ref[at, 128:256] = (last * cos[7]).astype(BF16)
+            one_ref[at, 256:384] = (-last * sin[7]).astype(BF16)
+            pairs = {4: (e4, -o4)}
+            for r in (1, 2, 3):
+                (er, ei), (br, bi), (c, s) = e[r - 1], o[r - 1], TURN[r]
+                tr, ti = c * br + s * bi, c * bi - s * br
+                pairs[r] = (er + tr, ei + ti)
+                pairs[8 - r] = (er - tr, ti - ei)
+            for r, (re, im) in pairs.items():
+                at = pl.ds((r - 1) * rows + w * n + lo, 16)
+                two_ref[at, 0:128] = (re * cos[r - 1] + im * sin[r - 1]).astype(BF16)
+                two_ref[at, 128:256] = (im * cos[r - 1] - re * sin[r - 1]).astype(BF16)
     moves[0].wait()
-    table = half(table_ref)
-    z_ref[:, 0:256] = dot(one_ref[...], table[0:256])
-    z_ref[:, 256:512] = dot(four_ref[...], table)
-    table = whole(table_ref)
-    y = dot(two_ref[...], table)
-    for m in range(3):
-        z_ref[:, 512 * (m + 1) : 512 * (m + 2)] = y[m * rows : (m + 1) * rows]
+    whole, ends = tables(table_ref)
+    z_ref[:, 0:256] = dot(one_ref[...], ends)
+    y = dot(two_ref[...], whole)
+    for r in range(1, 8):
+        z_ref[:, 256 * r : 256 * (r + 1)] = y[(r - 1) * rows : r * rows]
     total = None
     for re, im in COLS:
         zr, zi = z_ref[:, re : re + LANES], z_ref[:, im : im + LANES]
@@ -115,19 +124,16 @@
 
 
 def backward(one_ref, two_ref, h_ref, n, table_ref, tw_ref):
-    table = half_inverse(table_ref)
-    h_ref[:, 0:256] = dot(one_ref[pl.ds(0, n), :], table[:, 0:256])
-    y = dot(one_ref[pl.ds(n, n), :], table)
-    h_ref[:, 256:512] = y[:, 0:256] * tw_ref[3:4, :] + y[:, 256:512] * tw_ref[7:8, :]
-    table = whole(table_ref)
-    whole_y = dot(two_ref[...], table)
-    for m in range(3):
-        y = whole_y[m * n : (m + 1) * n]
-        re, minus_im = y[:, 0:256], y[:, 256:512]
-        cos, sin = tw_ref[m : m + 1, :], tw_ref[m + 4 : m + 5, :]
-        col = 512 * (m + 1)
-        h_ref[:, col : col + 256] = re * cos + minus_im * sin
-        h_ref[:, col + 256 : col + 512] = re * sin - minus_im * cos
+    whole, ends = tables(table_ref)
+    y = dot_t(one_ref[...], ends)
+    h_ref[:, 0:128] = y[:, 0:128]
+    h_ref[:, 128:256] = y[:, 128:256] * tw_ref[7:8, :] - y[:, 256:384] * tw_ref[15:16, :]
+    y = dot_t(two_ref[...], whole)
+    for r in range(1, 8):
+        re, im = y[(r - 1) * n : r * n, 0:128], y[(r - 1) * n : r * n, 128:256]
+        cos, sin = tw_ref[r - 1 : r, :], tw_ref[r + 7 : r + 8, :]
+        h_ref[:, 256 * r : 256 * r + 128] = re * cos - im * sin
+        h_ref[:, 256 * r + 128 : 256 * (r + 1)] = re * sin + im * cos
 
 
 def whitened(z_ref, level, re, im):
@@ -140,27 +146,34 @@
 def put(one_ref, two_ref, chunk, lo, sr, si):
     n = sr.shape[0]
     sr, si = (sr * (1.0 / 64)).astype(BF16), (si * (1.0 / 64)).astype(BF16)
-    if chunk < 2:
-        rows = pl.ds(chunk * (one_ref.shape[0] // 2) + lo, n)
-        one_ref[rows, 0:LANES] = sr
-        one_ref[rows, LANES : 2 * LANES] = -si
+    if chunk == 0:
+        one_ref[pl.ds(lo, n), 0:LANES] = sr
+        one_ref[pl.ds(lo, n), LANES : 2 * LANES] = si
     else:
-        rows = pl.ds((chunk - 2) // 2 * (two_ref.shape[0] // 3) + lo, n)
-        at = chunk % 2 * LANES
-        two_ref[rows, at : at + LANES] = sr
-        two_ref[rows, 256 + at : 256 + at + LANES] = -si
-
-
-def lags(h_ref, lo, n, half):
-    p0, p4, a2, b2, a1, b1, a3, b3 = (
-        h_ref[lo : lo + n, 256 * m + half * LANES : 256 * m + (half + 1) * LANES] for m in range(8)
-    )
+        rows = pl.ds((chunk - 1) * (two_ref.shape[0] // 7) + lo, n)
+        two_ref[rows, 0:LANES] = sr
+        two_ref[rows, LANES : 2 * LANES] = si
+
+
+def eight_lags(p0, p4, a1, b1, a2, b2, a3, b3):
     even, odd = p0 + p4, p0 - p4
     plus, minus = even + a2, even - a2
     a13, b31 = a1 + a3, b3 - b1
     low, high = odd - b2, odd + b2
     t1, t3 = C * (a1 - b1 - a3 - b3), C * (a3 - b3 - a1 - b1)
     return (plus + a13, low + t1, minus + b31, high + t3, plus - a13, low - t1, minus - b31, high - t3)
+
+
+def lags(h_ref, lo, n):
+    h = [h_ref[lo : lo + n, LANES * m : LANES * (m + 1)] for m in range(16)]
+    even, odd = [h[0] + h[1], h[8]], [h[0] - h[1], -h[9]]
+    for r in (1, 2, 3):
+        (ar, br), (al, bl), (c, s) = h[2 * r : 2 * r + 2], h[16 - 2 * r : 18 - 2 * r], TURN[r]
+        da, sb = ar - al, br + bl
+        even += [ar + al, br - bl]
+        odd += [c * da - s * sb, s * da + c * sb]
+    pairs = zip(eight_lags(*even), eight_lags(*odd))
+    return [lag for pair in pairs for lag in pair]
 
 
 NEAR, FAR, N = 48, 32, 80
@@ -189,7 +202,7 @@
 def correlate_kernel(dev_ref, partners_hbm, *refs):
     near_hbm, (recv_hbm, table_hbm, tw_hbm, near_out, far_out), refs = refs[:3], refs[3:8], refs[8:]
     near_refs, (recv_ref, table_ref, tw_ref, partners_ref), refs = refs[:3], refs[3:7], refs[7:]
-    x_ref, u1_ref, u4_ref, u2_ref, z_ref, w_ref, p_ref, s1_ref, s2_ref, h_ref, o_ref, near_ref, far_ref, sems, out_sems = refs
+    x_ref, u1_ref, u2_ref, z_ref, w_ref, p_ref, s1_ref, s2_ref, h_ref, o_ref, near_ref, far_ref, sems, out_sems = refs
     inputs = [*zip(near_hbm, near_refs), (recv_hbm, recv_ref)]
     moves = fetch([*inputs, (tw_hbm, tw_ref), (table_hbm, table_ref), (partners_hbm, partners_ref)], sems)
     x_ref[pl.ds(40 * STRIDE, 8 * STRIDE), :] = jnp.zeros((8 * STRIDE, LANES), F32)
@@ -199,7 +212,7 @@
         start = NEAR if ref is recv_ref else start
         spread(x_ref, STRIDE, start, ref, ref.shape[0] // ROWS)
         start += ref.shape[0] // ROWS
-    level = 0.1 * forward(x_ref, STRIDE, N, u1_ref, u4_ref, u2_ref, z_ref, table_ref, tw_ref, (moves[5], moves[4])) + 1e-6
+    level = 0.1 * forward(x_ref, STRIDE, N, u1_ref, u2_ref, z_ref, table_ref, tw_ref, (moves[5], moves[4])) + 1e-6
     for chunk, (re, im) in enumerate(COLS):
         wr, wi = whitened(z_ref, level, re, im)
         for w in range(2):
@@ -230,17 +243,14 @@
             put(s1_ref, s2_ref, chunk, c * 16, sr, si)
     backward(s1_ref, s2_ref, h_ref, PAIRS, table_ref, tw_ref)
     for lo in range(0, 64, 16):
-        for part in range(2):
-            for a, lag in enumerate(lags(h_ref, lo, 16, part)):
-                at = 256 * a + LANES * part
-                near_ref[lo : lo + 16, at : at + LANES] = lag.astype(BF16)
+        for a, lag in enumerate(lags(h_ref, lo, 16)):
+            near_ref[lo : lo + 16, LANES * a : LANES * (a + 1)] = lag.astype(BF16)
     outs = [pltpu.make_async_copy(near_ref, near_out, out_sems.at[0])]
     outs[0].start()
     for g in range(FAR // GROUP):
         for i in range(4):
-            for part in range(2):
-                for a, lag in enumerate(lags(h_ref, 64 + i * FAR + g * GROUP, GROUP, part)):
-                    o_ref[pl.ds(g * GROUP * SLOT + (2 * a + part) * 4 + i, GROUP, stride=SLOT), :] = lag
+            for a, lag in enumerate(lags(h_ref, 64 + i * FAR + g * GROUP, GROUP)):
+                o_ref[pl.ds(g * GROUP * SLOT + a * 4 + i, GROUP, stride=SLOT), :] = lag
         for s in range(g * GROUP, (g + 1) * GROUP):
             far_ref[pl.ds(s * 64, 64), :] = o_ref[pl.ds(s * SLOT, 64), :].astype(BF16)
         rows = pl.ds(g * GROUP * 64, GROUP * 64)
@@ -292,8 +302,8 @@
     arrived = lax.all_to_all(outgoing.reshape(16, 2 * ROWS, LANES), "grp", 0, 0, tiled=True).reshape(32 * ROWS, LANES)
 
     chip = jnp.concatenate([raw, other], axis=0)
+    two_side = lax.ppermute(chip, "dev", toward(2))
     one_side = lax.ppermute(chip, "dev", toward(1))
-    two_side = lax.ppermute(chip, "dev", toward(2))
     side = jnp.concatenate([one_side, two_side], axis=0)
     far_side = lax.ppermute(side, "dev", swap)
     dev = lax.axis_index("dev").astype(jnp.int32).reshape(1)
@@ -308,14 +318,13 @@
             pltpu.VMEM(twiddles.shape, F32),
             pltpu.SMEM((4, 16), jnp.int32),
             pltpu.VMEM((N * STRIDE, LANES), F32),
-            pltpu.VMEM((2 * N, 256), BF16),
-            pltpu.VMEM((2 * N, 512), BF16),
-            pltpu.VMEM((6 * N, 512), BF16),
+            pltpu.VMEM((2 * N, 384), BF16),
+            pltpu.VMEM((14 * N, 256), BF16),
             pltpu.VMEM((2 * N, NT), F32),
             pltpu.VMEM((2, NEAR, NT), BF16),
             pltpu.VMEM((2, 64, NT), F32),
-            pltpu.VMEM((2 * PAIRS, 256), BF16),
-            pltpu.VMEM((3 * PAIRS, 512), BF16),
+            pltpu.VMEM((PAIRS, 256), BF16),
+            pltpu.VMEM((7 * PAIRS, 256), BF16),
             pltpu.VMEM((PAIRS, NT), F32),
             pltpu.VMEM((FAR * SLOT, LANES), F32),
             pltpu.VMEM((64, NT), BF16),

time: 42.1 us -> 42 us (level)
  no operation moved by 1% of the time
where the time goes in v2:
time: 42 us; the launch traced here: 41.6 us
  starting transfers between devices  27.7 us (66%)
  Pallas kernels  6.27 us (15%)
  waiting for transfers between devices  6.14 us (15%)
  local copies, waits for them, and re-layouts  0.78 us (2%)
  between operations  0.72 us (2%)
    all_to_all x1, starting transfers between devices, shards(): lax.all_to_all(outgoing.reshape(16, 2 * ROWS, LANES), 'grp', 0, 0, tiled=...  14.7 us
    pallas_call x1, Pallas kernels, shards(): pl.pallas_call(correlate_kernel, out_shape=(like(64, NT), like(64 * FAR,...  4.59 us
    ppermute x1, starting transfers between devices, shards(): one_side = lax.ppermute(chip, 'dev', toward(1))  4.55 us
    ppermute x1, waiting for transfers between devices, shards(): two_side = lax.ppermute(chip, 'dev', toward(2))  4.34 us
    ppermute x1, starting transfers between devices, shards(): other = lax.ppermute(raw, 'dev', swap)  3.14 us
    ppermute x1, starting transfers between devices, shards(): far_side = lax.ppermute(side, 'dev', swap)  2.89 us
    ppermute x1, starting transfers between devices, shards(): two_side = lax.ppermute(chip, 'dev', toward(2))  2.43 us
    pallas_call x1, Pallas kernels, shards(): pl.pallas_call(select_kernel, out_shape=like(32 * ROWS, LANES), in_specs=...  1.68 us
  transfers between devices with their start and end apart: 5, of which 3 were waited for; matrix products, arithmetic and copies ran while one was open for 0% of the time, Pallas kernels for 0%

profile of v2, /device:TPU:57, one launch (start us, length us, event | category | flops | bytes accessed | tf_op | source)
XLA Modules:
  0.0 41.6 jit_solution(17092878123556750224)
XLA Ops:
  0.6 1.7 %select.1 = bf16[1024,128]{1,0:T(8,128)(2,1)} custom-call(s32[2,4]{1,0:T(2,128)} %bitcast.20, bf16[128,128]{1,0:T(8,128)(2,1)} %bitcast.17), custom_call_target="tpu_custom_call" | custom-call | tf_op jit(solution)/shard_map/select/pallas_call | solution.py:289
  2.3 0.0 copy-start.4
  2.3 14.7 %all-to-all-start = ((bf16[16,64,128]{2,1,0:T(8,128)(2,1)}), bf16[16,64,128]{2,1,0:T(8,128)(2,1)S(1)}, u32[]{:S(2)}, u32[]{:S(2)}) async-start(bf16[16,64,128]{2,1,0:T(8,128)(2,1)} %bitcast.16), calls=%async_computation | async-start | bytes 524288 | tf_op jit(solution)/shard_map/all_to_all | solution.py:302
  17.0 0.0 copy-done.4
  17.0 3.1 %collective-permute-start = (bf16[128,128]{1,0:T(8,128)(2,1)S(1)}, bf16[128,128]{1,0:T(8,128)(2,1)S(1)}, u32[]{:S(2)}, u32[]{:S(2)}) collective-permute-start(bf16[128,128]{1,0:T(8,128)(2,1)S(1)} %bitcast.18), channel_id=1, source_target_pairs={{0,1},{1,0},{2,3},{3,2},{4,5},{5,4},{6,7},{7,6},{8,9},{9,8},{10,11... | collective-permute-start | bytes 98312 | tf_op jit(solution)/shard_map/ppermute | solution.py:301
  20.1 0.8 %collective-permute-done = bf16[128,128]{1,0:T(8,128)(2,1)S(1)} collective-permute-done((bf16[128,128]{1,0:T(8,128)(2,1)S(1)}, bf16[128,128]{1,0:T(8,128)(2,1)S(1)}, u32[]{:S(2)}, u32[]{:S(2)}) %collective-permute-start) | collective-permute-done | bytes 32800 | tf_op jit(solution)/shard_map/ppermute | solution.py:301
  21.0 0.0 copy-start.2
  21.0 4.6 %collective-permute-start.1 = (bf16[256,128]{1,0:T(8,128)(2,1)S(1)}, bf16[256,128]{1,0:T(8,128)(2,1)S(1)}, u32[]{:S(2)}, u32[]{:S(2)}) collective-permute-start(bf16[256,128]{1,0:T(8,128)(2,1)S(1)} %pad_maximum_fusion.refs_0_), channel_id=1, source_target_pairs={{0,2},{2,4},{3,1},{4,6},{5,3},{6,8},{7,5},{8,10},{9,7},{10,12},{11... | collective-permute-start | bytes 196616 | tf_op jit(solution)/shard_map/ppermute | solution.py:306
  25.6 2.4 %collective-permute-start.2 = (bf16[256,128]{1,0:T(8,128)(2,1)S(1)}, bf16[256,128]{1,0:T(8,128)(2,1)S(1)}, u32[]{:S(2)}, u32[]{:S(2)}) collective-permute-start(bf16[256,128]{1,0:T(8,128)(2,1)S(1)} %pad_maximum_fusion.refs_0_), channel_id=1, source_target_pairs={{0,4},{2,6},{4,8},{5,1},{6,10},{7,3},{8,12},{9,5},{10,14},{11,7},{... | collective-permute-start | bytes 196616 | tf_op jit(solution)/shard_map/ppermute | solution.py:305
  28.0 0.0 collective-permute-done.1
  28.0 0.0 copy-done.2
  28.0 4.3 %collective-permute-done.2 = bf16[256,128]{1,0:T(8,128)(2,1)S(1)} collective-permute-done((bf16[256,128]{1,0:T(8,128)(2,1)S(1)}, bf16[256,128]{1,0:T(8,128)(2,1)S(1)}, u32[]{:S(2)}, u32[]{:S(2)}) %collective-permute-start.2) | collective-permute-done | bytes 65568 | tf_op jit(solution)/shard_map/ppermute | solution.py:305
  32.4 0.0 copy-start.1
  32.4 2.9 %collective-permute-start.3 = (bf16[512,128]{1,0:T(8,128)(2,1)S(1)}, bf16[512,128]{1,0:T(8,128)(2,1)S(1)}, u32[]{:S(2)}, u32[]{:S(2)}) collective-permute-start(bf16[512,128]{1,0:T(8,128)(2,1)S(1)} %constant_dynamic-update-slice_fusion.refs_1_), channel_id=1, source_target_pairs={{0,1},{1,0},{2,3},{3,2},{4,5},{5,4},{6,7},{7,6},{8,9},{9,8},{10,11... | collective-permute-start | bytes 393224 | tf_op jit(solution)/shard_map/ppermute | solution.py:308
  35.3 1.0 %collective-permute-done.3.refs_2_ = bf16[512,128]{1,0:T(8,128)(2,1)S(1)} collective-permute-done((bf16[512,128]{1,0:T(8,128)(2,1)S(1)}, bf16[512,128]{1,0:T(8,128)(2,1)S(1)}, u32[]{:S(2)}, u32[]{:S(2)}) %collective-permute-start.3) | collective-permute-done | bytes 131104 | tf_op jit(solution)/shard_map/ppermute | solution.py:308
  36.3 0.0 copy-start.3
  36.3 0.0 all-to-all-done
  36.3 0.0 copy-start
  36.3 0.0 copy-done.1
  36.3 0.6 %copy-done.3 = bf16[512,128]{1,0:T(8,128)(2,1)} copy-done((bf16[512,128]{1,0:T(8,128)(2,1)}, bf16[512,128]{1,0:T(8,128)(2,1)S(1)}, u32[]{:S(2)}) %copy-start.3) | copy-done | bytes 131096
  36.9 0.1 copy-done
  37.0 4.6 %correlate.1 = (bf16[64,2048]{1,0:T(8,128)(2,1)}, bf16[2048,128]{1,0:T(8,128)(2,1)}) custom-call(s32[1]{0:T(128)} %bitcast.dev_ref, s32[4,16]{1,0:T(4,128)} %partners_hbm.1, bf16[256,128]{1,0:T(8,128)(2,1)} %copy-done.2, bf16[512,128]{1,0:T(8,128)(2,1)} %copy-done.1, bf16[512,128]{1,0:T(8,128)(2,1)} %copy-done.3, bf16[1024,128]{1,0:T(8,128)(2,1)} %bitcast.15, ...), custom_call_target="tpu_custom_call" | custom-call | tf_op jit(solution)/shard_map/correlate/pallas_call | solution.py:311
  (3 shorter events, 0.0 us)
Async XLA Ops:
  2.3 14.7 %copy-start.4 = (bf16[4,2,2048]{2,1,0:T(2,128)(2,1)S(1)}, bf16[4,2,2048]{2,1,0:T(2,128)(2,1)}, u32[]{:S(2)}) copy-start(bf16[4,2,2048]{2,1,0:T(2,128)(2,1)} %param.5) | copy-start | bytes 98308
  2.3 33.9 %all-to-all-start = ((bf16[16,64,128]{2,1,0:T(8,128)(2,1)}), bf16[16,64,128]{2,1,0:T(8,128)(2,1)S(1)}, u32[]{:S(2)}, u32[]{:S(2)}) async-start(bf16[16,64,128]{2,1,0:T(8,128)(2,1)} %bitcast.16), calls=%async_computation | async-start | bytes 524288 | tf_op jit(solution)/shard_map/all_to_all | solution.py:302
  17.0 4.0 %collective-permute-start = (bf16[128,128]{1,0:T(8,128)(2,1)S(1)}, bf16[128,128]{1,0:T(8,128)(2,1)S(1)}, u32[]{:S(2)}, u32[]{:S(2)}) collective-permute-start(bf16[128,128]{1,0:T(8,128)(2,1)S(1)} %bitcast.18), channel_id=1, source_target_pairs={{0,1},{1,0},{2,3},{3,2},{4,5},{5,4},{6,7},{7,6},{8,9},{9,8},{10,11... | collective-permute-start | bytes 98312 | tf_op jit(solution)/shard_map/ppermute | solution.py:301
  21.0 7.0 %copy-start.2 = (bf16[256,128]{1,0:T(8,128)(2,1)}, bf16[256,128]{1,0:T(8,128)(2,1)S(1)}, u32[]{:S(2)}) copy-start(bf16[256,128]{1,0:T(8,128)(2,1)S(1)} %pad_maximum_fusion.refs_0_) | copy-start | bytes 196612
  21.0 7.0 %collective-permute-start.1 = (bf16[256,128]{1,0:T(8,128)(2,1)S(1)}, bf16[256,128]{1,0:T(8,128)(2,1)S(1)}, u32[]{:S(2)}, u32[]{:S(2)}) collective-permute-start(bf16[256,128]{1,0:T(8,128)(2,1)S(1)} %pad_maximum_fusion.refs_0_), channel_id=1, source_target_pairs={{0,2},{2,4},{3,1},{4,6},{5,3},{6,8},{7,5},{8,10},{9,7},{10,12},{11... | collective-permute-start | bytes 196616 | tf_op jit(solution)/shard_map/ppermute | solution.py:306
  25.6 6.8 %collective-permute-start.2 = (bf16[256,128]{1,0:T(8,128)(2,1)S(1)}, bf16[256,128]{1,0:T(8,128)(2,1)S(1)}, u32[]{:S(2)}, u32[]{:S(2)}) collective-permute-start(bf16[256,128]{1,0:T(8,128)(2,1)S(1)} %pad_maximum_fusion.refs_0_), channel_id=1, source_target_pairs={{0,4},{2,6},{4,8},{5,1},{6,10},{7,3},{8,12},{9,5},{10,14},{11,7},{... | collective-permute-start | bytes 196616 | tf_op jit(solution)/shard_map/ppermute | solution.py:305
  32.4 3.9 %copy-start.1 = (bf16[512,128]{1,0:T(8,128)(2,1)}, bf16[512,128]{1,0:T(8,128)(2,1)S(1)}, u32[]{:S(2)}) copy-start(bf16[512,128]{1,0:T(8,128)(2,1)S(1)} %constant_dynamic-update-slice_fusion.refs_1_) | copy-start | bytes 393220
  32.4 3.9 %collective-permute-start.3 = (bf16[512,128]{1,0:T(8,128)(2,1)S(1)}, bf16[512,128]{1,0:T(8,128)(2,1)S(1)}, u32[]{:S(2)}, u32[]{:S(2)}) collective-permute-start(bf16[512,128]{1,0:T(8,128)(2,1)S(1)} %constant_dynamic-update-slice_fusion.refs_1_), channel_id=1, source_target_pairs={{0,1},{1,0},{2,3},{3,2},{4,5},{5,4},{6,7},{7,6},{8,9},{9,8},{10,11... | collective-permute-start | bytes 393224 | tf_op jit(solution)/shard_map/ppermute | solution.py:308
  36.3 0.6 %copy-start.3 = (bf16[512,128]{1,0:T(8,128)(2,1)}, bf16[512,128]{1,0:T(8,128)(2,1)S(1)}, u32[]{:S(2)}) copy-start(bf16[512,128]{1,0:T(8,128)(2,1)S(1)} %collective-permute-done.3.refs_2_) | copy-start | bytes 393220
  36.3 0.7 %copy-start = (bf16[16,64,128]{2,1,0:T(8,128)(2,1)}, bf16[16,64,128]{2,1,0:T(8,128)(2,1)S(1)}, u32[]{:S(2)}) copy-start(bf16[16,64,128]{2,1,0:T(8,128)(2,1)S(1)} %all-to-all-done) | copy-start | bytes 786436

commit v3 on v2

--- a/solution.py
+++ b/solution.py
@@ -33,7 +33,7 @@
     return table.astype(np.float32).astype(jnp.bfloat16), twiddles
 
 
-VMEM_LIMIT = 60 * 1024 * 1024
+VMEM_LIMIT = 20 * 1024 * 1024
 
 
 def dot(a, b):
@@ -112,9 +112,8 @@
     moves[0].wait()
     whole, ends = tables(table_ref)
     z_ref[:, 0:256] = dot(one_ref[...], ends)
-    y = dot(two_ref[...], whole)
     for r in range(1, 8):
-        z_ref[:, 256 * r : 256 * (r + 1)] = y[(r - 1) * rows : r * rows]
+        z_ref[:, 256 * r : 256 * (r + 1)] = dot(two_ref[pl.ds((r - 1) * rows, rows), :], whole)
     total = None
     for re, im in COLS:
         zr, zi = z_ref[:, re : re + LANES], z_ref[:, im : im + LANES]
@@ -128,9 +127,11 @@
     y = dot_t(one_ref[...], ends)
     h_ref[:, 0:128] = y[:, 0:128]
     h_ref[:, 128:256] = y[:, 128:256] * tw_ref[7:8, :] - y[:, 256:384] * tw_ref[15:16, :]
-    y = dot_t(two_ref[...], whole)
+    c, s = whole[0:LANES, 0:LANES], whole[LANES:256, 0:LANES]
+    back = jnp.concatenate([jnp.concatenate([c, s], axis=1), jnp.concatenate([-s, c], axis=1)], axis=0)
     for r in range(1, 8):
-        re, im = y[(r - 1) * n : r * n, 0:128], y[(r - 1) * n : r * n, 128:256]
+        y = dot(two_ref[pl.ds((r - 1) * n, n), :], back)
+        re, im = y[:, 0:128], y[:, 128:256]
         cos, sin = tw_ref[r - 1 : r, :], tw_ref[r + 7 : r + 8, :]
         h_ref[:, 256 * r : 256 * r + 128] = re * cos - im * sin
         h_ref[:, 256 * r + 128 : 256 * (r + 1)] = re * sin + im * cos

time: 42 us -> 40.8 us (0.971)
  local copies, waits for them, and re-layouts: 0.78 us -> 0.04 us
  Pallas kernels: 6.27 us -> 5.65 us
    unnamed x11 -> x9, local copies, waits for them, and re-layouts: 0.76 us -> 0.03 us
    pallas_call x1, Pallas kernels: 4.59 us -> 3.97 us  [shards(): pl.pallas_call(correlate_kernel, out_shape=(like(64, NT), like(64 * FAR,...]
where the time goes in v3:
time: 40.8 us; the launch traced here: 40.4 us
  starting transfers between devices  27.8 us (68%)
  waiting for transfers between devices  6.15 us (15%)
  Pallas kernels  5.65 us (14%)
  between operations  0.72 us (2%)
    all_to_all x1, starting transfers between devices, shards(): lax.all_to_all(outgoing.reshape(16, 2 * ROWS, LANES), 'grp', 0, 0, tiled=...  14.7 us
    ppermute x1, starting transfers between devices, shards(): one_side = lax.ppermute(chip, 'dev', toward(1))  4.55 us
    ppermute x1, waiting for transfers between devices, shards(): two_side = lax.ppermute(chip, 'dev', toward(2))  4.35 us
    pallas_call x1, Pallas kernels, shards(): pl.pallas_call(correlate_kernel, out_shape=(like(64, NT), like(64 * FAR,...  3.97 us
    ppermute x1, starting transfers between devices, shards(): other = lax.ppermute(raw, 'dev', swap)  3.28 us
    ppermute x1, starting transfers between devices, shards(): far_side = lax.ppermute(side, 'dev', swap)  2.89 us
    ppermute x1, starting transfers between devices, shards(): two_side = lax.ppermute(chip, 'dev', toward(2))  2.43 us
    pallas_call x1, Pallas kernels, shards(): pl.pallas_call(select_kernel, out_shape=like(32 * ROWS, LANES), in_specs=...  1.68 us
  transfers between devices with their start and end apart: 5, of which 3 were waited for; matrix products, arithmetic and copies ran while one was open for 0% of the time, Pallas kernels for 0%

profile of v3, /device:TPU:57, one launch (start us, length us, event | category | flops | bytes accessed | tf_op | source)
XLA Modules:
  0.0 40.4 jit_solution(8835994268229100845)
XLA Ops:
  0.6 1.7 %select.1 = bf16[1024,128]{1,0:T(8,128)(2,1)} custom-call(s32[2,4]{1,0:T(2,128)} %bitcast.20, bf16[128,128]{1,0:T(8,128)(2,1)} %bitcast.17), custom_call_target="tpu_custom_call" | custom-call | tf_op jit(solution)/shard_map/select/pallas_call | solution.py:290
  2.3 0.0 copy-start.3
  2.3 14.7 %all-to-all-start = ((bf16[16,64,128]{2,1,0:T(8,128)(2,1)}), bf16[16,64,128]{2,1,0:T(8,128)(2,1)S(1)}, u32[]{:S(2)}, u32[]{:S(2)}) async-start(bf16[16,64,128]{2,1,0:T(8,128)(2,1)} %bitcast.16), calls=%async_computation | async-start | bytes 524288 | tf_op jit(solution)/shard_map/all_to_all | solution.py:303
  17.0 0.0 copy-done.3
  17.0 0.0 copy-start
  17.0 3.3 %collective-permute-start = (bf16[128,128]{1,0:T(8,128)(2,1)S(1)}, bf16[128,128]{1,0:T(8,128)(2,1)S(1)}, u32[]{:S(2)}, u32[]{:S(2)}) collective-permute-start(bf16[128,128]{1,0:T(8,128)(2,1)S(1)} %bitcast.18), channel_id=1, source_target_pairs={{0,1},{1,0},{2,3},{3,2},{4,5},{5,4},{6,7},{7,6},{8,9},{9,8},{10,11... | collective-permute-start | bytes 98312 | tf_op jit(solution)/shard_map/ppermute | solution.py:302
  20.3 0.8 %collective-permute-done = bf16[128,128]{1,0:T(8,128)(2,1)S(1)} collective-permute-done((bf16[128,128]{1,0:T(8,128)(2,1)S(1)}, bf16[128,128]{1,0:T(8,128)(2,1)S(1)}, u32[]{:S(2)}, u32[]{:S(2)}) %collective-permute-start) | collective-permute-done | bytes 32800 | tf_op jit(solution)/shard_map/ppermute | solution.py:302
  21.1 4.6 %collective-permute-start.1 = (bf16[256,128]{1,0:T(8,128)(2,1)S(1)}, bf16[256,128]{1,0:T(8,128)(2,1)S(1)}, u32[]{:S(2)}, u32[]{:S(2)}) collective-permute-start(bf16[256,128]{1,0:T(8,128)(2,1)S(1)} %pad_maximum_fusion.refs_0_), channel_id=1, source_target_pairs={{0,2},{2,4},{3,1},{4,6},{5,3},{6,8},{7,5},{8,10},{9,7},{10,12},{11... | collective-permute-start | bytes 196616 | tf_op jit(solution)/shard_map/ppermute | solution.py:307
  25.7 2.4 %collective-permute-start.2 = (bf16[256,128]{1,0:T(8,128)(2,1)S(1)}, bf16[256,128]{1,0:T(8,128)(2,1)S(1)}, u32[]{:S(2)}, u32[]{:S(2)}) collective-permute-start(bf16[256,128]{1,0:T(8,128)(2,1)S(1)} %pad_maximum_fusion.refs_0_), channel_id=1, source_target_pairs={{0,4},{2,6},{4,8},{5,1},{6,10},{7,3},{8,12},{9,5},{10,14},{11,7},{... | collective-permute-start | bytes 196616 | tf_op jit(solution)/shard_map/ppermute | solution.py:306
  28.1 0.0 collective-permute-done.1
  28.2 4.3 %collective-permute-done.2 = bf16[256,128]{1,0:T(8,128)(2,1)S(1)} collective-permute-done((bf16[256,128]{1,0:T(8,128)(2,1)S(1)}, bf16[256,128]{1,0:T(8,128)(2,1)S(1)}, u32[]{:S(2)}, u32[]{:S(2)}) %collective-permute-start.2) | collective-permute-done | bytes 65568 | tf_op jit(solution)/shard_map/ppermute | solution.py:306
  32.5 0.0 copy-start.2
  32.5 0.0 copy-start.1
  32.5 2.9 %collective-permute-start.3 = (bf16[512,128]{1,0:T(8,128)(2,1)S(1)}, bf16[512,128]{1,0:T(8,128)(2,1)S(1)}, u32[]{:S(2)}, u32[]{:S(2)}) collective-permute-start(bf16[512,128]{1,0:T(8,128)(2,1)S(1)} %constant_dynamic-update-slice_fusion.refs_1_), channel_id=1, source_target_pairs={{0,1},{1,0},{2,3},{3,2},{4,5},{5,4},{6,7},{7,6},{8,9},{9,8},{10,11... | collective-permute-start | bytes 393224 | tf_op jit(solution)/shard_map/ppermute | solution.py:309
  35.4 1.0 %collective-permute-done.3.refs_2_ = bf16[512,128]{1,0:T(8,128)(2,1)S(1)} collective-permute-done((bf16[512,128]{1,0:T(8,128)(2,1)S(1)}, bf16[512,128]{1,0:T(8,128)(2,1)S(1)}, u32[]{:S(2)}, u32[]{:S(2)}) %collective-permute-start.3) | collective-permute-done | bytes 131104 | tf_op jit(solution)/shard_map/ppermute | solution.py:309
  36.4 0.0 all-to-all-done
  36.4 0.0 copy-done
  36.4 0.0 copy-done.2
  36.4 0.0 copy-done.1
  36.4 4.0 %correlate.1 = (bf16[64,2048]{1,0:T(8,128)(2,1)}, bf16[2048,128]{1,0:T(8,128)(2,1)}) custom-call(s32[1]{0:T(128)} %bitcast.dev_ref, s32[4,16]{1,0:T(4,128)S(1)} %copy-done.2, bf16[256,128]{1,0:T(8,128)(2,1)S(1)} %pad_maximum_fusion.refs_0_, bf16[512,128]{1,0:T(8,128)(2,1)S(1)} %constant_dynamic-update-slice_fusion.refs_1_, ...), custom_call_target="tpu_custom_call" | custom-call | tf_op jit(solution)/shard_map/correlate/pallas_call | solution.py:312
  (3 shorter events, 0.0 us)
Async XLA Ops:
  2.3 14.7 %copy-start.3 = (bf16[4,2,2048]{2,1,0:T(2,128)(2,1)S(1)}, bf16[4,2,2048]{2,1,0:T(2,128)(2,1)}, u32[]{:S(2)}) copy-start(bf16[4,2,2048]{2,1,0:T(2,128)(2,1)} %param.5) | copy-start | bytes 98308
  2.3 34.1 %all-to-all-start = ((bf16[16,64,128]{2,1,0:T(8,128)(2,1)}), bf16[16,64,128]{2,1,0:T(8,128)(2,1)S(1)}, u32[]{:S(2)}, u32[]{:S(2)}) async-start(bf16[16,64,128]{2,1,0:T(8,128)(2,1)} %bitcast.16), calls=%async_computation | async-start | bytes 524288 | tf_op jit(solution)/shard_map/all_to_all | solution.py:303
  17.0 19.4 %copy-start = (bf16[1280,128]{1,0:T(8,128)(2,1)S(1)}, bf16[1280,128]{1,0:T(8,128)(2,1)}, u32[]{:S(2)}) copy-start(bf16[1280,128]{1,0:T(8,128)(2,1)} %constant.8.clone.refs_4_) | copy-start | bytes 983044
  17.0 4.1 %collective-permute-start = (bf16[128,128]{1,0:T(8,128)(2,1)S(1)}, bf16[128,128]{1,0:T(8,128)(2,1)S(1)}, u32[]{:S(2)}, u32[]{:S(2)}) collective-permute-start(bf16[128,128]{1,0:T(8,128)(2,1)S(1)} %bitcast.18), channel_id=1, source_target_pairs={{0,1},{1,0},{2,3},{3,2},{4,5},{5,4},{6,7},{7,6},{8,9},{9,8},{10,11... | collective-permute-start | bytes 98312 | tf_op jit(solution)/shard_map/ppermute | solution.py:302
  21.1 7.0 %collective-permute-start.1 = (bf16[256,128]{1,0:T(8,128)(2,1)S(1)}, bf16[256,128]{1,0:T(8,128)(2,1)S(1)}, u32[]{:S(2)}, u32[]{:S(2)}) collective-permute-start(bf16[256,128]{1,0:T(8,128)(2,1)S(1)} %pad_maximum_fusion.refs_0_), channel_id=1, source_target_pairs={{0,2},{2,4},{3,1},{4,6},{5,3},{6,8},{7,5},{8,10},{9,7},{10,12},{11... | collective-permute-start | bytes 196616 | tf_op jit(solution)/shard_map/ppermute | solution.py:307
  25.7 6.8 %collective-permute-start.2 = (bf16[256,128]{1,0:T(8,128)(2,1)S(1)}, bf16[256,128]{1,0:T(8,128)(2,1)S(1)}, u32[]{:S(2)}, u32[]{:S(2)}) collective-permute-start(bf16[256,128]{1,0:T(8,128)(2,1)S(1)} %pad_maximum_fusion.refs_0_), channel_id=1, source_target_pairs={{0,4},{2,6},{4,8},{5,1},{6,10},{7,3},{8,12},{9,5},{10,14},{11,7},{... | collective-permute-start | bytes 196616 | tf_op jit(solution)/shard_map/ppermute | solution.py:306
  32.5 3.9 %copy-start.2 = (s32[4,16]{1,0:T(4,128)S(1)}, s32[4,16]{1,0:T(4,128)}, u32[]{:S(2)}) copy-start(s32[4,16]{1,0:T(4,128)} %partners_hbm.1) | copy-start | bytes 772
  32.5 3.9 %copy-start.1 = (f32[16,128]{1,0:T(8,128)S(1)}, f32[16,128]{1,0:T(8,128)}, u32[]{:S(2)}) copy-start(f32[16,128]{1,0:T(8,128)} %constant.9.clone.refs_5_) | copy-start | bytes 24580
  32.5 3.9 %collective-permute-start.3 = (bf16[512,128]{1,0:T(8,128)(2,1)S(1)}, bf16[512,128]{1,0:T(8,128)(2,1)S(1)}, u32[]{:S(2)}, u32[]{:S(2)}) collective-permute-start(bf16[512,128]{1,0:T(8,128)(2,1)S(1)} %constant_dynamic-update-slice_fusion.refs_1_), channel_id=1, source_target_pairs={{0,1},{1,0},{2,3},{3,2},{4,5},{5,4},{6,7},{7,6},{8,9},{9,8},{10,11... | collective-permute-start | bytes 393224 | tf_op jit(solution)/shard_map/ppermute | solution.py:309
